TPU v7x, 512 devices: a whole 4x4x16 slice. The times are simulated.
512 devices in a mesh: seq: 128 (over x, z, core), ctx: 4 (over y).
Axes of the slice: x: 4, y: 4, z: 16, core: 2. Of those that a mesh axis runs over, the one named last changes fastest.
Arguments:
- hidden_rows: bfloat16 [128, 256, 8192], P('seq', 'ctx'), may hold values from -6 to 6
- chosen_query_rows: bfloat16 [128, 256, 8192], P('seq', 'ctx'), may hold values from -160 to 160
- key_rows: bfloat16 [128, 256, 1024], P('seq', 'ctx'), may hold values from -7 to 7
- chosen_value_rows: bfloat16 [128, 256, 1024], P('seq', 'ctx'), may hold values from -6 to 6
- output_gradient: bfloat16 [128, 256, 8192], P('seq', 'ctx'), may hold values from -6 to 6
- positions: int32 [128, 256], P('seq', 'ctx'), may hold values from 0 to 2048, as said below
- counts: int32 [128, 4], P('seq', 'ctx'), may hold values from 16 to 64, as said below
- router: float32 [8192], replicated, may hold values from -0.0625 to 0.0625
Outputs:
- query_gradient: bfloat16 [128, 256, 8192], P('seq', 'ctx')
- key_gradient: bfloat16 [128, 256, 1024], P('seq', 'ctx')
- value_gradient: bfloat16 [128, 256, 1024], P('seq', 'ctx')
- router_grad: float32 [8192], replicated
Inputs may be any that keep to these rules, and one draw needn't show every extreme that they name: `counts`: some device holds 64 live rows in every draw. On device j of ctx, slots 0 to counts - 1 hold distinct increasing positions from j * 512 to (j + 1) * 512 - 1; the other slots hold 2048.
All inputs are finite; a program needn't handle non-finite values.
Results may differ from a plain program's by a relative error of at most 0.024.
Values may be sent and summed in bfloat16 or wider, within the bound.
No kernel may reach another device: no remote copies, remote signals or barrier semaphores. Data moves between devices by JAX's collectives and lax.ppermute only.
A program may use at most 64 MiB of HBM per device.

v0:
```python
import math

import jax
import jax.numpy as jnp
from jax import lax
from jax.sharding import PartitionSpec as P

QUERY_HEADS = 64
KEY_VALUE_HEADS = 8
HEAD_SIZE = 128


def head_scores(query_head_rows, key_head_rows, scale):
    return (
        jnp.einsum(
            "qhgd,khd->hgqk", query_head_rows, key_head_rows, preferred_element_type=jnp.float32
        )
        * scale
    )


def body(
    hidden_rows,
    chosen_query_rows,
    key_rows,
    chosen_value_rows,
    output_gradient,
    positions,
    counts,
    router,
):
    slot_capacity = chosen_query_rows.shape[1]
    query_group_width = QUERY_HEADS // KEY_VALUE_HEADS
    scale = 1.0 / math.sqrt(HEAD_SIZE)
    valid = (jnp.arange(slot_capacity) < counts[0, 0]).astype(jnp.float32)
    hidden = hidden_rows[0].astype(jnp.float32)
    logits = jnp.dot(hidden, router, precision=lax.Precision.HIGHEST)
    sigma = jax.nn.sigmoid(logits)
    gate = sigma * valid
    gathered_keys, gathered_values = (
        lax.all_gather(key_rows, "ctx", axis=1, tiled=True),
        lax.all_gather(chosen_value_rows, "ctx", axis=1, tiled=True),
    )
    key_places = lax.all_gather(positions, "ctx", axis=1, tiled=True)[0]
    own_places = positions[0]
    query_head_rows = chosen_query_rows[0].reshape(
        slot_capacity, KEY_VALUE_HEADS, query_group_width, HEAD_SIZE
    )
    key_head_rows = gathered_keys[0].reshape(-1, KEY_VALUE_HEADS, HEAD_SIZE)
    value_head_rows = gathered_values[0].reshape(-1, KEY_VALUE_HEADS, HEAD_SIZE)
    scores = head_scores(query_head_rows, key_head_rows, scale)
    allowed = key_places[None, :] <= own_places[:, None]
    scores = jnp.where(allowed, scores, -1e30)
    row_max = jnp.max(scores, axis=-1)
    weights = jnp.exp(scores - row_max[..., None])
    row_sum = jnp.sum(weights, axis=-1)
    probs = (weights / row_sum[..., None]).astype(jnp.bfloat16)
    attended = jnp.einsum(
        "hgqk,khd->qhgd", probs, value_head_rows, preferred_element_type=jnp.float32
    )
    gradient_list = (
        output_gradient[0]
        .reshape(slot_capacity, KEY_VALUE_HEADS, query_group_width, HEAD_SIZE)
        .astype(jnp.float32)
    )
    grad_attended = (gate[:, None, None, None] * gradient_list).astype(jnp.bfloat16)
    logit_grad = jnp.sum(gradient_list * attended, axis=(1, 2, 3)) * sigma * (1.0 - sigma) * valid
    row_dot = jnp.transpose(
        jnp.sum(grad_attended.astype(jnp.float32) * attended, axis=-1), (1, 2, 0)
    )
    grad_probs = jnp.einsum(
        "qhgd,khd->hgqk", grad_attended, value_head_rows, preferred_element_type=jnp.float32
    )
    grad_scores = (probs.astype(jnp.float32) * (grad_probs - row_dot[..., None])).astype(
        jnp.bfloat16
    )
    query_part = (
        jnp.einsum("hgqk,khd->qhgd", grad_scores, key_head_rows, preferred_element_type=jnp.float32)
        * scale
    )
    query_gradient = query_part.astype(jnp.bfloat16).reshape(
        1, slot_capacity, QUERY_HEADS * HEAD_SIZE
    )
    value_portion = jnp.einsum(
        "hgqk,qhgd->khd", probs, grad_attended, preferred_element_type=jnp.float32
    )
    key_portion = (
        jnp.einsum(
            "hgqk,qhgd->khd", grad_scores, query_head_rows, preferred_element_type=jnp.float32
        )
        * scale
    )
    key_gradient, value_gradient = (
        lax.psum_scatter(
            key_portion.reshape(1, -1, KEY_VALUE_HEADS * HEAD_SIZE),
            "ctx",
            scatter_dimension=1,
            tiled=True,
        ),
        lax.psum_scatter(
            value_portion.reshape(1, -1, KEY_VALUE_HEADS * HEAD_SIZE),
            "ctx",
            scatter_dimension=1,
            tiled=True,
        ),
    )
    rows_total = lax.axis_size("seq") * lax.axis_size("ctx") * slot_capacity
    router_factor = jnp.dot(logit_grad, hidden, precision=lax.Precision.HIGHEST) / math.sqrt(
        rows_total
    )
    router_grad = lax.psum(router_factor, ("seq", "ctx"))
    return (
        query_gradient,
        key_gradient.astype(jnp.bfloat16),
        value_gradient.astype(jnp.bfloat16),
        router_grad,
    )


def solution(mesh):
    placed = (
        P("seq", "ctx", None),
        P("seq", "ctx", None),
        P("seq", "ctx", None),
        P("seq", "ctx", None),
        P("seq", "ctx", None),
        P("seq", "ctx"),
        P("seq", "ctx"),
        P(),
    )
    return jax.shard_map(
        body,
        mesh=mesh,
        in_specs=placed,
        out_specs=(P("seq", "ctx", None), P("seq", "ctx", None), P("seq", "ctx", None), P()),
        check_vma=False,
    )
```

profile of v0, /device:TPU:1, one launch (start us, length us, event | category | flops | bytes accessed | tf_op | source)
XLA Modules:
  0.0 192.2 jit_solution(16546684643817907096)
XLA Ops:
  7.2 0.0 copy-start
  7.2 0.0 copy-start.9
  7.2 0.0 copy-start.8
  7.2 0.0 reduce-scatter.3.cloned.1.call-start
  7.3 11.6 %all_gather.10 = bf16[1,256,1024]{2,1,0:T(8,128)(2,1)S(1)} all-gather(bf16[1,64,1024]{2,1,0:T(8,128)(2,1)} %param.10), channel_id=1, replica_groups=mesh['seq'=128,'ctx'=4] {'ctx'}, dimensions={1}, use_global_device_ids=true | all-gather | bytes 655360 | tf_op jit(solution)/shard_map/all_gather | solution.py:41
  18.8 0.2 copy.33
  19.1 0.0 copy-start.6
  19.1 1.7 copy.60
  20.8 0.0 copy-start.1
  20.8 1.3 dynamic-slice
  22.8 0.0 copy-done.9
  22.8 0.1 bitcast_dynamic-update-slice_fusion
  22.9 6.2 %all-reduce = s32[256]{0:T(256)S(1)} all-reduce(s32[256]{0:T(256)S(1)} %bitcast_dynamic-update-slice_fusion), channel_id=1, replica_groups=mesh['seq'=128,'ctx'=4] {'ctx'}, use_global_device_ids=true, to_apply=%add | all-reduce | flops 256 | bytes 2048
  29.7 0.0 copy-done.8
  29.7 10.2 %all_gather.11 = bf16[1,256,1024]{2,1,0:T(8,128)(2,1)S(1)} all-gather(bf16[1,64,1024]{2,1,0:T(8,128)(2,1)S(1)} %copy-done.8), channel_id=1, replica_groups=mesh['seq'=128,'ctx'=4] {'ctx'}, dimensions={1}, use_global_device_ids=true | all-gather | bytes 655360 | tf_op jit(solution)/shard_map/all_gather | solution.py:42
  39.9 1.0 copy.37
  40.9 1.4 convert_bitcast_fusion
  42.3 0.4 copy.61
  42.7 0.0 copy-done.6
  42.7 0.0 copy-done.1
  42.7 0.9 fusion.19
  43.6 0.1 broadcast_compare_fusion
  43.6 1.9 fusion.33
  45.5 0.0 copy-start.10
  45.5 0.0 copy-start.7
  45.5 0.7 divide_convert_fusion
  46.3 0.0 copy-done
  46.3 0.0 copy-done.10
  46.3 0.9 compare_select_fusion.1
  47.2 0.0 copy-done.7
  47.2 1.8 fusion.5
  49.0 0.0 copy-start.5
  49.0 0.0 copy-start.2
  49.0 0.9 fusion.2
  50.0 0.1 copy-done.5
  50.0 0.6 copy-done.2
  50.6 0.0 copy-start.3
  50.6 2.5 %fusion.10 = f32[8,256,128]{1,2,0:T(8,128)} fusion(bf16[8,8,64,256]{3,2,1,0:T(8,128)(2,1)S(1)} %fusion.2, bf16[64,8,8,128]{3,2,1,0:T(8,128)(2,1)S(1)} %bitcast.104), kind=kOutput, calls=%fused_computation.20 | convolution fusion | flops 268697600 | bytes 4194304 | tf_op jit(solution)/shard_map/hgqk,qhgd->khd/dot_general | solution.py:88
  53.1 0.0 copy-done.3
  53.1 2.5 %copy.43 = f32[1,256,1024]{2,1,0:T(8,128)} copy(f32[1,256,1024]{1,2,0:T(8,128)} %bitcast.106) | data formatting | bytes 2097152 | tf_op jit(solution)/shard_map/reshape | solution.py:95
  55.7 0.0 reduce-scatter.3.cloned.1.call-update
  55.7 0.2 reduce-scatter.5.cloned.1.call-start
  55.9 2.7 %fusion.34 = f32[8,128,256,1]{2,1,3,0:T(8,128)} fusion(bf16[64,8,8,128]{3,0,2,1:T(8,128)(2,1)} %copy-done.5, bf16[8,8,64,256]{3,2,1,0:T(8,128)(2,1)S(1)} %divide_convert_fusion), kind=kOutput, calls=%fused_computation.49 | convolution fusion | flops 268435456 | bytes 4194304 | tf_op jit(solution)/shard_map/hgqk,qhgd->khd/dot_general | solution.py:84
  58.7 0.0 copy-start.4
  58.7 2.7 %copy.44 = f32[1,256,1024]{2,1,0:T(8,128)} copy(f32[1,256,1024]{1,2,0:T(8,128)} %bitcast.105) | data formatting | bytes 2097152 | tf_op jit(solution)/shard_map/reshape | solution.py:101
  61.4 0.0 reduce-scatter.5.cloned.1.call-update
  61.4 0.0 copy-done.4
  61.4 1.7 fusion.9
  63.1 0.7 copy.41
  63.8 1.3 reshape.24
  65.1 0.5 fusion.15
  65.6 116.5 %psum.7 = f32[8192]{0:T(1024)} all-reduce(f32[8192]{0:T(1024)S(1)} %broadcast_multiply_fusion), channel_id=1, replica_groups=mesh['seq'=128,'ctx'=4] {'seq','ctx'}, use_global_device_ids=true, to_apply=%region_6.7 | all-reduce | flops 8192 | bytes 65536 | tf_op jit(solution)/shard_map/psum | solution.py:111
  182.1 0.0 reduce-scatter.3.cloned.1.call-done
  182.1 1.6 convert_element_type.44
  183.7 0.0 reduce-scatter.5.cloned.1.call-done
  183.7 1.6 convert_element_type.45
  (2 shorter events, 0.0 us)
Async XLA Ops:
  7.2 39.1 %copy-start = (bf16[1,64,8192]{2,1,0:T(8,128)(2,1)S(1)}, bf16[1,64,8192]{2,1,0:T(8,128)(2,1)}, u32[]{:S(2)}) copy-start(bf16[1,64,8192]{2,1,0:T(8,128)(2,1)} %param.8) | copy-start | bytes 3145732
  7.2 15.6 %copy-start.9 = (s32[1,64]{1,0:T(1,128)S(1)}, s32[1,64]{1,0:T(1,128)}, u32[]{:S(2)}) copy-start(s32[1,64]{1,0:T(1,128)} %param.13) | copy-start | bytes 772
  7.2 22.5 %copy-start.8 = (bf16[1,64,1024]{2,1,0:T(8,128)(2,1)S(1)}, bf16[1,64,1024]{2,1,0:T(8,128)(2,1)}, u32[]{:S(2)}) copy-start(bf16[1,64,1024]{2,1,0:T(8,128)(2,1)} %param.11) | copy-start | bytes 393220
  7.2 174.9 %reduce-scatter.3.cloned.1.call-start = ((), (), s32[]{:S(2)}) async-start(), calls=%async_computation.2 | async-start | bytes 1310720 | tf_op jit(solution)/shard_map/reduce_scatter | solution.py:94
  19.1 23.6 %copy-start.6 = (bf16[1,256,1024]{1,2,0:T(8,128)(2,1)}, bf16[1,256,1024]{1,2,0:T(8,128)(2,1)S(1)}, u32[]{:S(2)}) copy-start(bf16[1,256,1024]{1,2,0:T(8,128)(2,1)S(1)} %copy.33) | copy-start | bytes 1572868
  20.8 21.9 %copy-start.1 = (bf16[8,8,64,128]{3,2,1,0:T(8,128)(2,1)}, bf16[8,8,64,128]{3,2,1,0:T(8,128)(2,1)S(1)}, u32[]{:S(2)}) copy-start(bf16[8,8,64,128]{3,2,1,0:T(8,128)(2,1)S(1)} %copy.60) | copy-start | bytes 3145732
  45.5 0.8 copy-start.10
  45.5 1.7 copy-start.7
  49.0 1.0 copy-start.5
  49.0 1.6 copy-start.2
  50.6 2.5 %copy-start.3 = (bf16[8,8,64,256]{3,2,1,0:T(8,128)(2,1)}, bf16[8,8,64,256]{3,2,1,0:T(8,128)(2,1)S(1)}, u32[]{:S(2)}) copy-start(bf16[8,8,64,256]{3,2,1,0:T(8,128)(2,1)S(1)} %fusion.2) | copy-start | bytes 6291460
  55.7 128.0 %reduce-scatter.5.cloned.1.call-start = ((), (), s32[]{:S(2)}) async-start(), calls=%async_computation.3 | async-start | bytes 1310720 | tf_op jit(solution)/shard_map/reduce_scatter | solution.py:100
  58.7 2.7 %copy-start.4 = (bf16[8,8,64,256]{3,2,1,0:T(8,128)(2,1)S(1)}, bf16[8,8,64,256]{3,2,1,0:T(8,128)(2,1)}, u32[]{:S(2)}) copy-start(bf16[8,8,64,256]{3,2,1,0:T(8,128)(2,1)} %copy-done.3) | copy-start | bytes 6291460
Sparse Core Ops, SparseCore 0:
  55.8 40.9 reduce-scatter.2
  99.9 31.0 reduce-scatter.4
where the time goes:
time: 193 us; the launch traced here: 192 us
  blocking collectives  144 us (75%)
  between operations  15.6 us (8%)
  local copies, waits for them, and re-layouts  12.6 us (7%)
  matrix products  12 us (6%)
  other arithmetic  7.27 us (4%)
    psum x1, blocking collectives, body(): router_grad = lax.psum(router_factor, ('seq', 'ctx'))  116 us
    all_gather x1, blocking collectives, body(): lax.all_gather(key_rows, 'ctx', axis=1, tiled=True)  11.6 us
    all_gather x1, blocking collectives, body(): lax.all_gather(chosen_value_rows, 'ctx', axis=1, tiled=True)  10.2 us
    unnamed x1, blocking collectives  6.19 us
    unnamed x27, local copies, waits for them, and re-layouts  4.22 us
  transfers between devices with their start and end apart: 2, of which 0 were waited for; matrix products, arithmetic and copies ran while one was open for 6% of the time, Pallas kernels for 0%

commit v1 on v0

v1 whole, which is shorter than its diff:
```python
import functools
import math

import jax
import jax.numpy as jnp
from jax import lax
from jax.experimental import pallas as pl
from jax.experimental.pallas import tpu as pltpu
from jax.sharding import Mesh, PartitionSpec as P

QUERY_HEADS = 64
KEY_VALUE_HEADS = 8
HEAD_SIZE = 128
GROUP = QUERY_HEADS // KEY_VALUE_HEADS
KV_WIDTH = KEY_VALUE_HEADS * HEAD_SIZE
SCALE = 1.0 / math.sqrt(HEAD_SIZE)
LOG2_SCALE = SCALE * math.log2(math.e)
X, Z, CORES, Y = 4, 16, 2, 4
PLANE = X * CORES * Y
VMEM_LIMIT = 48 * 1024 * 1024
NT = (((1,), (1,)), ((), ()))
TN = (((0,), (0,)), ((), ()))
NN = (((1,), (0,)), ((), ()))


def dot(a, b, dims):
    return lax.dot_general(a, b, dims, preferred_element_type=jnp.float32)


def params():
    return pltpu.CompilerParams(vmem_limit_bytes=VMEM_LIMIT)


def column(row, rows):
    wide = jnp.broadcast_to(row, (rows, rows))
    diagonal = lax.broadcasted_iota(jnp.int32, (rows, rows), 0) == lax.broadcasted_iota(
        jnp.int32, (rows, rows), 1
    )
    return jnp.sum(jnp.where(diagonal, wide.astype(jnp.float32), 0.0), axis=1, keepdims=True)


def pack_kernel(key_ref, value_ref, place_ref, out_ref):
    rows = key_ref.shape[1]
    places = column(place_ref[...], rows)
    high = jnp.floor(places * (1.0 / 16.0))
    low = places - 16.0 * high
    lane = lax.broadcasted_iota(jnp.int32, (rows, 128), 1)
    coded = jnp.where(lane == 0, high, jnp.where(lane == 1, low, 0.0)).astype(jnp.bfloat16)
    for part in range(Y):
        out_ref[part, :, :KV_WIDTH] = key_ref[0]
        out_ref[part, :, KV_WIDTH : 2 * KV_WIDTH] = value_ref[0]
        out_ref[part, :, 2 * KV_WIDTH :] = coded


def gate_kernel(hidden_ref, router_ref, count_ref, gate_ref, slope_ref):
    rows, width = hidden_ref.shape[1:]
    step = 1024
    total = jnp.zeros((rows, 128), jnp.float32)
    for start in range(0, width, step):
        product = hidden_ref[0, :, start : start + step].astype(jnp.float32) * router_ref[
            :, start : start + step
        ]
        for piece in range(0, step, 128):
            total = total + product[:, piece : piece + 128]
    logits = jnp.sum(total, axis=1, keepdims=True)
    sigma = jax.nn.sigmoid(logits)
    slot = lax.broadcasted_iota(jnp.int32, (rows, 1), 0)
    valid = (slot < count_ref[0, 0]).astype(jnp.float32)
    gate_ref[...] = jnp.broadcast_to(sigma * valid, (rows, 128))
    slope_ref[...] = jnp.broadcast_to(sigma * (1.0 - sigma) * valid, (rows, 128))


def key_places(place_block):
    coded = place_block.reshape(-1, 128).astype(jnp.float32)
    return coded[:, 0:1] * 16.0 + coded[:, 1:2]


def stack_heads(block, first, rows):
    return jnp.concatenate(
        [block[:, (first + g) * HEAD_SIZE : (first + g + 1) * HEAD_SIZE] for g in range(GROUP)],
        axis=0,
    )


def weights_of(keys, queries, allowed):
    scores = jnp.where(allowed, dot(keys, queries, NT), -1e30)
    top = jnp.max(scores, axis=0, keepdims=True)
    weights = jnp.exp2((scores - top) * LOG2_SCALE)
    return weights, jnp.sum(weights, axis=0, keepdims=True)


def forward_kernel(
    heads, q_ref, grad_ref, k_ref, v_ref, kp_ref, qp_ref, slope_ref, hidden_ref, out_ref, acc_ref
):
    step = pl.program_id(0)
    rows = q_ref.shape[1]
    across = GROUP * rows

    @pl.when(step == 0)
    def _():
        acc_ref[...] = jnp.zeros_like(acc_ref)

    allowed = key_places(kp_ref[...]) <= qp_ref[...].astype(jnp.float32)
    for c in range(heads):
        queries = stack_heads(q_ref[0], c * GROUP, rows)
        grads = stack_heads(grad_ref[0], c * GROUP, rows)
        keys = k_ref[:, :, c * HEAD_SIZE : (c + 1) * HEAD_SIZE].reshape(-1, HEAD_SIZE)
        values = v_ref[:, :, c * HEAD_SIZE : (c + 1) * HEAD_SIZE].reshape(-1, HEAD_SIZE)
        weights, total = weights_of(keys, queries, allowed)
        along = dot(values, grads, NT)
        acc_ref[...] += jnp.sum(weights * along, axis=0, keepdims=True) / total

    @pl.when(step == pl.num_programs(0) - 1)
    def _():
        per_head = acc_ref[...]
        row_sum = per_head[:, :rows]
        for g in range(1, GROUP):
            row_sum = row_sum + per_head[:, g * rows : (g + 1) * rows]
        wide = jnp.broadcast_to(row_sum, (rows, rows))
        diagonal = lax.broadcasted_iota(jnp.int32, (rows, rows), 0) == lax.broadcasted_iota(
            jnp.int32, (rows, rows), 1
        )
        down = jnp.sum(jnp.where(diagonal, wide, 0.0), axis=1, keepdims=True)
        logit_grad = down * slope_ref[:, :1] * (1.0 / math.sqrt(X * Z * CORES * Y * rows))
        chunk = out_ref.shape[2]
        for part in range(PLANE):
            block = hidden_ref[0, :, part * chunk : (part + 1) * chunk].astype(jnp.float32)
            out_ref[part] = jnp.sum(block * logit_grad, axis=0, keepdims=True)


def backward_kernel(
    heads, q_ref, grad_ref, k_ref, v_ref, kp_ref, qp_ref, gate_ref, dq_ref, dk_ref, dv_ref
):
    rows = q_ref.shape[1]
    blocks = k_ref.shape[0]
    allowed = key_places(kp_ref[...]) <= qp_ref[...].astype(jnp.float32)
    gate = gate_ref[:, :1]
    for c in range(heads):
        queries = stack_heads(q_ref[0], c * GROUP, rows)
        grads = jnp.concatenate(
            [
                (
                    grad_ref[
                        0, :, (c * GROUP + g) * HEAD_SIZE : (c * GROUP + g + 1) * HEAD_SIZE
                    ].astype(jnp.float32)
                    * gate
                ).astype(jnp.bfloat16)
                for g in range(GROUP)
            ],
            axis=0,
        )
        own = slice(c * HEAD_SIZE, (c + 1) * HEAD_SIZE)
        keys = k_ref[:, :, own].reshape(-1, HEAD_SIZE)
        values = v_ref[:, :, own].reshape(-1, HEAD_SIZE)
        weights, total = weights_of(keys, queries, allowed)
        probs = (weights * (1.0 / total)).astype(jnp.bfloat16)
        probs32 = probs.astype(jnp.float32)
        grad_probs = dot(values, grads, NT)
        row_dot = jnp.sum(probs32 * grad_probs, axis=0, keepdims=True)
        grad_scores = (probs32 * (grad_probs - row_dot)).astype(jnp.bfloat16)
        dv = dot(probs, grads, NN)
        dk = dot(grad_scores, queries, NN) * SCALE
        dq = dot(grad_scores, keys, TN) * SCALE
        dv_ref[:, :, own] = dv.astype(jnp.bfloat16).reshape(blocks, rows, HEAD_SIZE)
        dk_ref[:, :, own] = dk.astype(jnp.bfloat16).reshape(blocks, rows, HEAD_SIZE)
        dq = dq.astype(jnp.bfloat16)
        for g in range(GROUP):
            left = (c * GROUP + g) * HEAD_SIZE
            dq_ref[0, :, left : left + HEAD_SIZE] = dq[g * rows : (g + 1) * rows]


def body(
    hidden_rows,
    chosen_query_rows,
    key_rows,
    chosen_value_rows,
    output_gradient,
    positions,
    counts,
    router,
):
    rows, width = chosen_query_rows.shape[1:]
    payload = pl.pallas_call(
        pack_kernel,
        out_shape=jax.ShapeDtypeStruct((Y, rows, 2 * KV_WIDTH + 128), jnp.bfloat16),
        compiler_params=params(),
        name="pack",
    )(key_rows, chosen_value_rows, positions)
    gathered = lax.all_to_all(payload, "ctx", 0, 0, tiled=True)

    gate, slope = pl.pallas_call(
        gate_kernel,
        out_shape=[jax.ShapeDtypeStruct((rows, 128), jnp.float32)] * 2,
        in_specs=[
            pl.BlockSpec(memory_space=pltpu.VMEM),
            pl.BlockSpec(memory_space=pltpu.VMEM),
            pl.BlockSpec(memory_space=pltpu.SMEM),
        ],
        compiler_params=params(),
        cost_estimate=pl.CostEstimate(
            flops=2 * rows * width, bytes_accessed=2 * rows * width, transcendentals=rows
        ),
        name="gate",
    )(hidden_rows, router.reshape(1, width), counts)

    query_places = jnp.tile(positions, (1, GROUP))
    heads = 2
    steps = KEY_VALUE_HEADS // heads
    span = heads * HEAD_SIZE
    wide_block = pl.BlockSpec((1, rows, heads * GROUP * HEAD_SIZE), lambda i: (0, 0, i))
    key_block = pl.BlockSpec((Y, rows, span), lambda i: (0, 0, i))
    value_block = pl.BlockSpec((Y, rows, span), lambda i: (0, 0, i + steps))
    place_block = pl.BlockSpec((Y, rows, 128), lambda i: (0, 0, 2 * KEY_VALUE_HEADS))

    def whole(*shape):
        return pl.BlockSpec(shape, lambda i: (0,) * len(shape))

    chunk = width // PLANE
    term = pl.pallas_call(
        functools.partial(forward_kernel, heads),
        grid=(steps,),
        out_shape=jax.ShapeDtypeStruct((PLANE, 1, chunk), jnp.float32),
        in_specs=[
            wide_block,
            wide_block,
            key_block,
            value_block,
            place_block,
            whole(1, GROUP * rows),
            whole(rows, 128),
            whole(1, rows, width),
        ],
        out_specs=whole(PLANE, 1, chunk),
        scratch_shapes=[pltpu.VMEM((1, GROUP * rows), jnp.float32)],
        compiler_params=params(),
        cost_estimate=pl.CostEstimate(
            flops=4 * rows * width * Y * rows,
            bytes_accessed=6 * rows * width,
            transcendentals=rows * QUERY_HEADS * Y * rows,
        ),
        name="forward",
    )(
        chosen_query_rows,
        output_gradient,
        gathered,
        gathered,
        gathered,
        query_places,
        slope,
        hidden_rows,
    )

    plane = ("x", "core", "ctx")
    shares = lax.all_to_all(term, plane, 0, 0, tiled=True)
    share = jnp.sum(shares, axis=0, keepdims=True)
    lines = lax.all_to_all(jnp.broadcast_to(share, (Z, 1, chunk)), "z", 0, 0, tiled=True)
    line = jnp.sum(lines, axis=0, keepdims=True)
    router_grad = lax.all_to_all(
        jnp.broadcast_to(line, (PLANE, 1, chunk)), plane, 0, 0, tiled=True
    ).reshape(width)

    part = pl.BlockSpec((Y, rows, span), lambda i: (0, 0, i))
    query_gradient, key_terms, value_terms = pl.pallas_call(
        functools.partial(backward_kernel, heads),
        grid=(steps,),
        out_shape=[
            jax.ShapeDtypeStruct((1, rows, width), jnp.bfloat16),
            jax.ShapeDtypeStruct((Y, rows, KV_WIDTH), jnp.bfloat16),
            jax.ShapeDtypeStruct((Y, rows, KV_WIDTH), jnp.bfloat16),
        ],
        in_specs=[
            wide_block,
            wide_block,
            key_block,
            value_block,
            place_block,
            whole(1, GROUP * rows),
            whole(rows, 128),
        ],
        out_specs=[wide_block, part, part],
        compiler_params=params(),
        cost_estimate=pl.CostEstimate(
            flops=10 * rows * width * Y * rows,
            bytes_accessed=6 * rows * width,
            transcendentals=rows * QUERY_HEADS * Y * rows,
        ),
        name="backward",
    )(
        chosen_query_rows,
        output_gradient,
        gathered,
        gathered,
        gathered,
        query_places,
        gate,
    )
    key_shares = lax.all_to_all(key_terms, "ctx", 0, 0, tiled=True)
    value_shares = lax.all_to_all(value_terms, "ctx", 0, 0, tiled=True)
    key_gradient = jnp.sum(key_shares.astype(jnp.float32), axis=0, keepdims=True)
    value_gradient = jnp.sum(value_shares.astype(jnp.float32), axis=0, keepdims=True)
    return (
        query_gradient,
        key_gradient.astype(jnp.bfloat16),
        value_gradient.astype(jnp.bfloat16),
        router_grad,
    )


def solution(mesh):
    fine = Mesh(mesh.devices.reshape(X, Z, CORES, Y), ("x", "z", "core", "ctx"))
    seq = ("x", "z", "core")
    rows3 = P(seq, "ctx", None)
    rows2 = P(seq, "ctx")
    return jax.shard_map(
        body,
        mesh=fine,
        in_specs=(rows3, rows3, rows3, rows3, rows3, rows2, rows2, P()),
        out_specs=(rows3, rows3, rows3, P()),
        check_vma=False,
    )
```

time: 193 us -> 110 us (0.57)
  blocking collectives: 144 us -> 57.5 us
  waiting for transfers between devices: 0.04 us -> 14.5 us
  between operations: 15.6 us -> 1.35 us
  starting transfers between devices: 0.26 us -> 13.9 us
  matrix products: 12 us -> 0 us
  Pallas kernels: 0 us -> 11.3 us
  other arithmetic: 7.27 us -> 1.58 us
  local copies, waits for them, and re-layouts: 12.6 us -> 7.84 us
    psum x1 -> x0, blocking collectives: 116 us -> none  [body(): router_grad = lax.psum(router_factor, ('seq', 'ctx'))]
    all_to_all x0 -> x3, blocking collectives: none -> 57.5 us  [the longest x1 26.1 us: body(): lax.all_to_all(jnp.broadcast_to(share, (Z, 1, chunk)), 'z', 0, 0, tiled=T...]
    all_gather x2 -> x0, blocking collectives: 21.8 us -> none  [the longest x1 11.6 us: body(): lax.all_gather(key_rows, 'ctx', axis=1, tiled=True)]
    all_to_all x0 -> x3, waiting for transfers between devices: none -> 14.5 us  [the longest x1 7.89 us: body(): gathered = lax.all_to_all(payload, 'ctx', 0, 0, tiled=True)]
    all_to_all x0 -> x3, starting transfers between devices: none -> 13.9 us  [the longest x1 5.32 us: body(): lax.all_to_all(jnp.broadcast_to(line, (PLANE, 1, chunk)), plane, 0, 0, ti...]
    dot_general x8 -> x0, matrix products: 12 us -> none  [the longest x1 2.73 us: body(): jnp.einsum('hgqk,qhgd->khd', probs, grad_attended, preferred_element_type...]
    pallas_call x0 -> x4, Pallas kernels: none -> 11.3 us  [the longest x1 6.65 us: body(): pl.pallas_call(functools.partial(backward_kernel, heads), grid=(steps,),...]
    reshape x3 -> x0, local copies, waits for them, and re-layouts: 6.51 us -> none  [the longest x1 2.69 us: body(): value_portion.reshape(1, -1, KEY_VALUE_HEADS * HEAD_SIZE)]
  transfers between devices with their start and end apart: 2 -> 3, of which waited for: 0 -> 2; matrix products, arithmetic and copies ran while one was open for 6% -> 1% of each run, Pallas kernels for 0% -> 6%
where the time goes in v1:
time: 110 us; the launch traced here: 108 us
  blocking collectives  57.5 us (52%)
  waiting for transfers between devices  14.5 us (13%)
  starting transfers between devices  13.9 us (13%)
  Pallas kernels  11.3 us (10%)
  local copies, waits for them, and re-layouts  7.84 us (7%)
  other arithmetic  1.58 us (1%)
  between operations  1.35 us (1%)
    all_to_all x1, blocking collectives, body(): lax.all_to_all(jnp.broadcast_to(share, (Z, 1, chunk)), 'z', 0, 0, tiled=T...  26.1 us
    all_to_all x1, blocking collectives, body(): shares = lax.all_to_all(term, plane, 0, 0, tiled=True)  18.6 us
    all_to_all x1, blocking collectives, body(): key_shares = lax.all_to_all(key_terms, 'ctx', 0, 0, tiled=True)  12.8 us
    all_to_all x1, waiting for transfers between devices, body(): gathered = lax.all_to_all(payload, 'ctx', 0, 0, tiled=True)  7.89 us
    unnamed x23, local copies, waits for them, and re-layouts  7.12 us
    pallas_call x1, Pallas kernels, body(): pl.pallas_call(functools.partial(backward_kernel, heads), grid=(steps,),...  6.65 us
    all_to_all x1, waiting for transfers between devices, body(): value_shares = lax.all_to_all(value_terms, 'ctx', 0, 0, tiled=True)  6.64 us
    all_to_all x1, starting transfers between devices, body(): lax.all_to_all(jnp.broadcast_to(line, (PLANE, 1, chunk)), plane, 0, 0, ti...  5.32 us
  transfers between devices with their start and end apart: 3, of which 2 were waited for; matrix products, arithmetic and copies ran while one was open for 1% of the time, Pallas kernels for 6%

profile of v1, /device:TPU:1, one launch (start us, length us, event | category | flops | bytes accessed | tf_op | source)
XLA Modules:
  0.0 108.1 jit_solution(12366677990879209142)
XLA Ops:
  0.6 0.0 copy-start.6
  0.6 0.9 copy-done.6
  1.5 0.0 copy-start.7
  1.5 0.9 copy-done.7
  2.4 0.0 copy-start.9
  2.4 0.7 copy-done.9
  3.1 1.1 %pack.1 = bf16[4,64,2176]{2,1,0:T(8,128)(2,1)} custom-call(bf16[1,64,1024]{2,1,0:T(8,128)(2,1)S(1)} %copy-done.6, bf16[1,64,1024]{2,1,0:T(8,128)(2,1)S(1)} %copy-done.7, s32[1,64]{1,0:T(1,128)S(1)} %copy-done.9), custom_call_target="tpu_custom_call" | custom-call | tf_op jit(solution)/shard_map/pack/pallas_call | solution.py:183
  4.2 0.0 copy-start.10
  4.2 0.0 copy-start.8
  4.2 0.0 copy-start
  4.2 0.0 copy-start.1
  4.2 5.2 %all-to-all-start = ((bf16[4,64,2176]{2,1,0:T(8,128)(2,1)}), bf16[4,64,2176]{2,1,0:T(8,128)(2,1)S(1)}, u32[]{:S(2)}, u32[]{:S(2)}) async-start(bf16[4,64,2176]{2,1,0:T(8,128)(2,1)} %pack.1), calls=%async_computation | async-start | bytes 2228224 | tf_op jit(solution)/shard_map/all_to_all | solution.py:189
  10.0 0.0 copy-done.10
  10.0 0.1 tile.13.qp_ref
  10.1 0.0 copy-done.8
  10.1 0.0 copy-start.2
  10.1 1.2 %copy-done.2 = bf16[1,64,8192]{2,1,0:T(8,128)(2,1)S(1)} copy-done((bf16[1,64,8192]{2,1,0:T(8,128)(2,1)S(1)}, bf16[1,64,8192]{2,1,0:T(8,128)(2,1)}, u32[]{:S(2)}) %copy-start.2) | copy-done | bytes 1048600
  11.3 0.3 gate.1
  11.6 7.9 %all-to-all-done.k_ref.v_ref.kp_ref = bf16[4,64,2176]{2,1,0:T(8,128)(2,1)S(1)} async-done(((bf16[4,64,2176]{2,1,0:T(8,128)(2,1)}), bf16[4,64,2176]{2,1,0:T(8,128)(2,1)S(1)}, u32[]{:S(2)}, u32[]{:S(2)}) %all-to-all-start) | async-done | bytes 1114144 | tf_op jit(solution)/shard_map/all_to_all | solution.py:189
  19.5 0.0 copy-done
  19.5 0.0 copy-done.1
  19.5 0.0 copy-start.3
  19.5 1.2 %copy-done.3 = bf16[1,64,8192]{2,1,0:T(8,128)(2,1)S(1)} copy-done((bf16[1,64,8192]{2,1,0:T(8,128)(2,1)S(1)}, bf16[1,64,8192]{2,1,0:T(8,128)(2,1)}, u32[]{:S(2)}) %copy-start.3) | copy-done | bytes 1048600
  20.8 3.3 %forward.1 = f32[32,1,256]{2,1,0:T(1,128)S(1)} custom-call(bf16[1,64,8192]{2,1,0:T(8,128)(2,1)S(1)} %copy-done, bf16[1,64,8192]{2,1,0:T(8,128)(2,1)S(1)} %copy-done.1, bf16[4,64,2176]{2,1,0:T(8,128)(2,1)S(1)} %all-to-all-done.k_ref.v_ref.kp_ref, bf16[4,64,2176]{2,1,0:T(8,128)(2,1)S(1)} %all-to-all-done.k_ref.v_ref.kp_ref, ...), custom_call_target="tpu_custom_call" | custom-call | flops 536870912 | bytes 3145728 | tf_op jit(solution)/shard_map/forward/pallas_call | solution.py:219
  24.0 18.6 %all_to_all.30 = f32[32,1,256]{2,1,0:T(1,128)S(1)} all-to-all(f32[32,1,256]{2,1,0:T(1,128)S(1)} %forward.1), channel_id=1, replica_groups=mesh['x'=4,'z'=16,'core'=2,'ctx'=4] {'x','core','ctx'}, dimensions={0} | all-to-all | bytes 65536 | tf_op jit(solution)/shard_map/all_to_all | solution.py:254
  42.7 0.1 reduce_sum.44
  42.8 26.1 %all_to_all.31 = f32[16,1,256]{2,1,0:T(1,128)S(1)} all-to-all(f32[16,1,256]{2,1,0:T(1,128)S(1)} %broadcast_in_dim.4), channel_id=1, replica_groups=mesh['x'=4,'z'=16,'core'=2,'ctx'=4] {'z'}, dimensions={0} | all-to-all | bytes 32768 | tf_op jit(solution)/shard_map/all_to_all | solution.py:256
  68.9 0.6 broadcast_in_dim.5
  69.5 5.3 %all-to-all-start.5 = ((f32[32,1,256]{2,1,0:T(1,128)}), f32[32,1,256]{2,1,0:T(1,128)S(1)}, u32[]{:S(2)}, u32[]{:S(2)}) async-start(f32[32,1,256]{2,1,0:T(1,128)} %broadcast_in_dim.5), calls=%async_computation.5 | async-start | bytes 65536 | tf_op jit(solution)/shard_map/all_to_all | solution.py:258
  74.9 6.7 %backward.1 = (bf16[1,64,8192]{2,1,0:T(8,128)(2,1)}, bf16[4,64,1024]{2,1,0:T(8,128)(2,1)S(1)}, bf16[4,64,1024]{2,1,0:T(8,128)(2,1)S(1)}) custom-call(bf16[1,64,8192]{2,1,0:T(8,128)(2,1)S(1)} %copy-done, bf16[1,64,8192]{2,1,0:T(8,128)(2,1)S(1)} %copy-done.1, bf16[4,64,2176]{2,1,0:T(8,128)(2,1)S(1)} %all-to-all-done.k_ref.v_ref.kp_ref, ...), custom_call_target="tpu_custom_call" | custom-call | flops 1342177280 | bytes 3145728 | tf_op jit(solution)/shard_map/backward/pallas_call | solution.py:263
  81.5 0.0 copy-start.4
  81.5 0.8 copy-done.4
  82.3 0.0 copy-start.5
  82.3 0.8 copy-done.5
  83.1 0.0 all-to-all-done.5
  83.1 12.8 %all_to_all.32 = bf16[4,64,1024]{2,1,0:T(8,128)(2,1)S(1)} all-to-all(bf16[4,64,1024]{2,1,0:T(8,128)(2,1)} %copy-done.5), channel_id=1, replica_groups=mesh['x'=4,'z'=16,'core'=2,'ctx'=4] {'ctx'}, dimensions={0} | all-to-all | bytes 1048576 | tf_op jit(solution)/shard_map/all_to_all | solution.py:297
  95.9 3.5 %all-to-all-start.2 = ((bf16[4,64,1024]{2,1,0:T(8,128)(2,1)}), bf16[4,64,1024]{2,1,0:T(8,128)(2,1)S(1)}, u32[]{:S(2)}, u32[]{:S(2)}) async-start(bf16[4,64,1024]{2,1,0:T(8,128)(2,1)} %copy-done.4), calls=%async_computation.2 | async-start | bytes 1048576 | tf_op jit(solution)/shard_map/all_to_all | solution.py:298
  99.4 0.7 reduce_sum.42
  100.1 6.6 %all-to-all-done.2 = bf16[4,64,1024]{2,1,0:T(8,128)(2,1)S(1)} async-done(((bf16[4,64,1024]{2,1,0:T(8,128)(2,1)}), bf16[4,64,1024]{2,1,0:T(8,128)(2,1)S(1)}, u32[]{:S(2)}, u32[]{:S(2)}) %all-to-all-start.2) | async-done | bytes 524320 | tf_op jit(solution)/shard_map/all_to_all | solution.py:298
  106.8 0.7 reduce_sum.43
  107.5 0.6 copy.16
  (3 shorter events, 0.1 us)
Async XLA Ops:
  0.6 0.9 copy-start.6
  1.5 0.9 copy-start.7
  2.4 0.7 copy-start.9
  4.2 5.8 %copy-start.10 = (s32[1,64]{1,0:T(1,128)S(1)}, s32[1,64]{1,0:T(1,128)}, u32[]{:S(2)}) copy-start(s32[1,64]{1,0:T(1,128)} %place_ref.1) | copy-start | bytes 772
  4.2 5.9 %copy-start.8 = (f32[8192]{0:T(1024)S(1)}, f32[8192]{0:T(1024)}, u32[]{:S(2)}) copy-start(f32[8192]{0:T(1024)} %param.15) | copy-start | bytes 98308
  4.2 15.3 %copy-start = (bf16[1,64,8192]{2,1,0:T(8,128)(2,1)S(1)}, bf16[1,64,8192]{2,1,0:T(8,128)(2,1)}, u32[]{:S(2)}) copy-start(bf16[1,64,8192]{2,1,0:T(8,128)(2,1)} %q_ref.3) | copy-start | bytes 3145732
  4.2 15.3 %copy-start.1 = (bf16[1,64,8192]{2,1,0:T(8,128)(2,1)S(1)}, bf16[1,64,8192]{2,1,0:T(8,128)(2,1)}, u32[]{:S(2)}) copy-start(bf16[1,64,8192]{2,1,0:T(8,128)(2,1)} %grad_ref.3) | copy-start | bytes 3145732
  4.2 15.3 %all-to-all-start = ((bf16[4,64,2176]{2,1,0:T(8,128)(2,1)}), bf16[4,64,2176]{2,1,0:T(8,128)(2,1)S(1)}, u32[]{:S(2)}, u32[]{:S(2)}) async-start(bf16[4,64,2176]{2,1,0:T(8,128)(2,1)} %pack.1), calls=%async_computation | async-start | bytes 2228224 | tf_op jit(solution)/shard_map/all_to_all | solution.py:189
  10.1 1.2 %copy-start.2 = (bf16[1,64,8192]{2,1,0:T(8,128)(2,1)S(1)}, bf16[1,64,8192]{2,1,0:T(8,128)(2,1)}, u32[]{:S(2)}) copy-start(bf16[1,64,8192]{2,1,0:T(8,128)(2,1)} %hidden_ref.3) | copy-start | bytes 3145732
  19.5 1.2 %copy-start.3 = (bf16[1,64,8192]{2,1,0:T(8,128)(2,1)S(1)}, bf16[1,64,8192]{2,1,0:T(8,128)(2,1)}, u32[]{:S(2)}) copy-start(bf16[1,64,8192]{2,1,0:T(8,128)(2,1)} %hidden_ref.3) | copy-start | bytes 3145732
  69.5 13.6 %all-to-all-start.5 = ((f32[32,1,256]{2,1,0:T(1,128)}), f32[32,1,256]{2,1,0:T(1,128)S(1)}, u32[]{:S(2)}, u32[]{:S(2)}) async-start(f32[32,1,256]{2,1,0:T(1,128)} %broadcast_in_dim.5), calls=%async_computation.5 | async-start | bytes 65536 | tf_op jit(solution)/shard_map/all_to_all | solution.py:258
  81.5 0.8 copy-start.4
  82.3 0.8 copy-start.5
  95.9 10.9 %all-to-all-start.2 = ((bf16[4,64,1024]{2,1,0:T(8,128)(2,1)}), bf16[4,64,1024]{2,1,0:T(8,128)(2,1)S(1)}, u32[]{:S(2)}, u32[]{:S(2)}) async-start(bf16[4,64,1024]{2,1,0:T(8,128)(2,1)} %copy-done.4), calls=%async_computation.2 | async-start | bytes 1048576 | tf_op jit(solution)/shard_map/all_to_all | solution.py:298

commit v2 on v1

v2 whole, which is shorter than its diff:
```python
import functools
import math

import jax
import jax.numpy as jnp
from jax import lax
from jax.experimental import pallas as pl
from jax.experimental.pallas import tpu as pltpu
from jax.sharding import Mesh, PartitionSpec as P

QUERY_HEADS = 64
KEY_VALUE_HEADS = 8
HEAD_SIZE = 128
GROUP = QUERY_HEADS // KEY_VALUE_HEADS
KV_WIDTH = KEY_VALUE_HEADS * HEAD_SIZE
SCALE = 1.0 / math.sqrt(HEAD_SIZE)
LOG2_SCALE = SCALE * math.log2(math.e)
X, Z, CORES, Y = 4, 16, 2, 4
PLANE = X * CORES * Y
VMEM_LIMIT = 48 * 1024 * 1024
FULL_VMEM = 60 * 1024 * 1024
FOLD_FLOPS = 1 << 35
HBM = pl.BlockSpec(memory_space=pltpu.HBM)
NT = (((1,), (1,)), ((), ()))
TN = (((0,), (0,)), ((), ()))
NN = (((1,), (0,)), ((), ()))


def dot(a, b, dims):
    return lax.dot_general(a, b, dims, preferred_element_type=jnp.float32)


def params(limit=VMEM_LIMIT):
    return pltpu.CompilerParams(vmem_limit_bytes=limit)


def column(row, rows):
    wide = jnp.broadcast_to(row, (rows, rows))
    diagonal = lax.broadcasted_iota(jnp.int32, (rows, rows), 0) == lax.broadcasted_iota(
        jnp.int32, (rows, rows), 1
    )
    return jnp.sum(jnp.where(diagonal, wide.astype(jnp.float32), 0.0), axis=1, keepdims=True)


def pack_kernel(key_ref, value_ref, place_ref, out_ref, row_ref, block_ref, in_sems, out_sems):
    rows = key_ref.shape[1]
    fetches = [
        pltpu.make_async_copy(place_ref, row_ref, in_sems.at[0]),
        pltpu.make_async_copy(key_ref.at[0], block_ref.at[:, :KV_WIDTH], in_sems.at[1]),
        pltpu.make_async_copy(
            value_ref.at[0], block_ref.at[:, KV_WIDTH : 2 * KV_WIDTH], in_sems.at[2]
        ),
    ]
    for fetch in fetches:
        fetch.start()
    fetches[0].wait()
    places = column(row_ref[...], rows)
    high = jnp.floor(places * (1.0 / 16.0))
    low = places - 16.0 * high
    lane = lax.broadcasted_iota(jnp.int32, (rows, 128), 1)
    coded = jnp.where(lane == 0, high, jnp.where(lane == 1, low, 0.0))
    block_ref[:, 2 * KV_WIDTH :] = coded.astype(jnp.bfloat16)
    fetches[1].wait()
    fetches[2].wait()
    copies = [
        pltpu.make_async_copy(block_ref, out_ref.at[part], out_sems.at[part]) for part in range(Y)
    ]
    for copy in copies:
        copy.start()
    for copy in copies:
        copy.wait()


def gate_kernel(hidden_ref, router_ref, count_ref, gate_ref, slope_ref):
    rows, width = hidden_ref.shape[1:]
    step = 1024
    total = jnp.zeros((rows, 128), jnp.float32)
    for start in range(0, width, step):
        product = hidden_ref[0, :, start : start + step].astype(jnp.float32) * router_ref[
            :, start : start + step
        ]
        for piece in range(0, step, 128):
            total = total + product[:, piece : piece + 128]
    logits = jnp.sum(total, axis=1, keepdims=True)
    sigma = jax.nn.sigmoid(logits)
    slot = lax.broadcasted_iota(jnp.int32, (rows, 1), 0)
    valid = (slot < count_ref[0, 0]).astype(jnp.float32)
    gate_ref[...] = jnp.broadcast_to(sigma * valid, (rows, 128))
    slope_ref[...] = jnp.broadcast_to(sigma * (1.0 - sigma) * valid, (rows, 128))


def key_places(place_block):
    coded = place_block.reshape(-1, 128).astype(jnp.float32)
    return coded[:, 0:1] * 16.0 + coded[:, 1:2]


def stack_heads(block, first, rows):
    return jnp.concatenate(
        [block[:, (first + g) * HEAD_SIZE : (first + g + 1) * HEAD_SIZE] for g in range(GROUP)],
        axis=0,
    )


def mask_bias(places, query_places):
    return jnp.where(places <= query_places.astype(jnp.float32), 0.0, -1e30)


def weights_of(keys, queries, bias):
    copies = GROUP * 64 // bias.shape[1]
    scores = dot(keys, queries, NT) + jnp.concatenate([bias] * copies, axis=1)
    top = jnp.max(scores, axis=0, keepdims=True)
    weights = jnp.exp2((scores - top) * LOG2_SCALE)
    return weights, jnp.sum(weights, axis=0, keepdims=True)


def forward_kernel(q_ref, grad_ref, pay_ref, qp_ref, out_ref):
    rows = q_ref.shape[1]
    bias = mask_bias(key_places(pay_ref[:, :, 2 * KV_WIDTH :]), qp_ref[:, : 2 * rows])
    acc = jnp.zeros((1, GROUP * rows), jnp.float32)
    for c in range(KEY_VALUE_HEADS):
        left = c * HEAD_SIZE
        queries = stack_heads(q_ref[0], c * GROUP, rows)
        grads = stack_heads(grad_ref[0], c * GROUP, rows)
        keys = pay_ref[:, :, left : left + HEAD_SIZE].reshape(-1, HEAD_SIZE)
        left = left + KV_WIDTH
        values = pay_ref[:, :, left : left + HEAD_SIZE].reshape(-1, HEAD_SIZE)
        weights, total = weights_of(keys, queries, bias)
        along = dot(values, grads, NT)
        acc = acc + jnp.sum(weights * along, axis=0, keepdims=True) / total
    row_sum = acc[:, :rows]
    for g in range(1, GROUP):
        row_sum = row_sum + acc[:, g * rows : (g + 1) * rows]
    wide = jnp.broadcast_to(row_sum, (rows, rows))
    diagonal = lax.broadcasted_iota(jnp.int32, (rows, rows), 0) == lax.broadcasted_iota(
        jnp.int32, (rows, rows), 1
    )
    down = jnp.sum(jnp.where(diagonal, wide, 0.0), axis=1, keepdims=True)
    out_ref[...] = jnp.broadcast_to(down, (rows, 128))


def router_kernel(along_ref, slope_ref, hidden_ref, out_ref):
    rows, chunk = hidden_ref.shape[1], out_ref.shape[2]
    logit_grad = along_ref[...] * slope_ref[...] * (1.0 / math.sqrt(X * Z * CORES * Y * rows))
    for part in range(PLANE):
        for lane in range(0, chunk, 128):
            left = part * chunk + lane
            block = hidden_ref[0, :, left : left + 128].astype(jnp.float32)
            out_ref[part, :, lane : lane + 128] = jnp.sum(
                block * logit_grad, axis=0, keepdims=True
            )


def backward_kernel(
    heads,
    q_ref,
    grad_ref,
    k_ref,
    v_ref,
    kp_ref,
    qp_ref,
    gate_ref,
    dq_ref,
    *term_refs,
):
    rows = q_ref.shape[1]
    me = lax.axis_index("ctx")
    owners = [lax.rem(me + Y - back, Y) for back in range(Y)]

    def blocks(ref, columns):
        return jnp.concatenate([ref[owner, :, columns] for owner in owners], axis=0)

    bias = mask_bias(key_places(blocks(kp_ref, slice(0, 128))), qp_ref[:, : 2 * rows])
    gate = gate_ref[:, :1]
    for c in range(heads):
        queries = stack_heads(q_ref[0], c * GROUP, rows)
        grads = jnp.concatenate(
            [
                (
                    grad_ref[
                        0, :, (c * GROUP + g) * HEAD_SIZE : (c * GROUP + g + 1) * HEAD_SIZE
                    ].astype(jnp.float32)
                    * gate
                ).astype(jnp.bfloat16)
                for g in range(GROUP)
            ],
            axis=0,
        )
        own = slice(c * HEAD_SIZE, (c + 1) * HEAD_SIZE)
        beside = slice((heads + c) * HEAD_SIZE, (heads + c + 1) * HEAD_SIZE)
        keys = blocks(k_ref, own)
        values = blocks(v_ref, own)
        weights, total = weights_of(keys, queries, bias)
        probs = (weights * (1.0 / total)).astype(jnp.bfloat16)
        probs32 = probs.astype(jnp.float32)
        grad_probs = dot(values, grads, NT)
        row_dot = jnp.sum(probs32 * grad_probs, axis=0, keepdims=True)
        grad_scores = (probs32 * (grad_probs - row_dot)).astype(jnp.bfloat16)
        dv = dot(probs, grads, NN).astype(jnp.bfloat16)
        dk = (dot(grad_scores, queries, NN) * SCALE).astype(jnp.bfloat16)
        dq = (dot(grad_scores, keys, TN) * SCALE).astype(jnp.bfloat16)
        for back, term_ref in enumerate(term_refs):
            term_ref[:, own] = dk[back * rows : (back + 1) * rows]
            term_ref[:, beside] = dv[back * rows : (back + 1) * rows]
        for g in range(GROUP):
            left = (c * GROUP + g) * HEAD_SIZE
            dq_ref[0, :, left : left + HEAD_SIZE] = dq[g * rows : (g + 1) * rows]


def combine_kernel(span, *refs):
    share_refs, (dk_ref, dv_ref) = refs[:-2], refs[-2:]
    total = share_refs[0][...].astype(jnp.float32)
    for share_ref in share_refs[1:]:
        total = total + share_ref[...].astype(jnp.float32)
    total = total.astype(jnp.bfloat16)
    for i in range(KV_WIDTH // span):
        own = slice(i * span, (i + 1) * span)
        dk_ref[0, :, own] = total[:, 2 * i * span : (2 * i + 1) * span]
        dv_ref[0, :, own] = total[:, (2 * i + 1) * span : (2 * i + 2) * span]


def fold_kernel(share_ref, out_ref):
    total = share_ref[0]
    for part in range(1, share_ref.shape[0]):
        total = total + share_ref[part]
    for part in range(out_ref.shape[0]):
        out_ref[part] = total


def fold(shares, parts, flops):
    return pl.pallas_call(
        fold_kernel,
        out_shape=jax.ShapeDtypeStruct((parts, *shares.shape[1:]), shares.dtype),
        compiler_params=params(),
        cost_estimate=pl.CostEstimate(flops=flops, bytes_accessed=4096, transcendentals=0),
        name="fold",
    )(shares)


def body(
    hidden_rows,
    chosen_query_rows,
    key_rows,
    chosen_value_rows,
    output_gradient,
    positions,
    counts,
    router,
):
    rows, width = chosen_query_rows.shape[1:]
    payload = pl.pallas_call(
        pack_kernel,
        out_shape=jax.ShapeDtypeStruct((Y, rows, 2 * KV_WIDTH + 128), jnp.bfloat16),
        in_specs=[HBM, HBM, HBM],
        out_specs=HBM,
        scratch_shapes=[
            pltpu.VMEM((1, rows), jnp.int32),
            pltpu.VMEM((rows, 2 * KV_WIDTH + 128), jnp.bfloat16),
            pltpu.SemaphoreType.DMA((3,)),
            pltpu.SemaphoreType.DMA((Y,)),
        ],
        compiler_params=params(FULL_VMEM),
        name="pack",
    )(key_rows, chosen_value_rows, positions)
    gathered = lax.all_to_all(payload, "ctx", 0, 0, tiled=True)

    gate, slope = pl.pallas_call(
        gate_kernel,
        out_shape=[jax.ShapeDtypeStruct((rows, 128), jnp.float32)] * 2,
        in_specs=[
            pl.BlockSpec(memory_space=pltpu.VMEM),
            pl.BlockSpec(memory_space=pltpu.VMEM),
            pl.BlockSpec(memory_space=pltpu.SMEM),
        ],
        compiler_params=params(FULL_VMEM),
        cost_estimate=pl.CostEstimate(
            flops=2 * rows * width, bytes_accessed=2 * rows * width, transcendentals=rows
        ),
        name="gate",
    )(hidden_rows, router.reshape(1, width), counts)

    query_places = jnp.tile(positions, (1, GROUP))
    heads = 2
    steps = KEY_VALUE_HEADS // heads
    span = heads * HEAD_SIZE
    wide_block = pl.BlockSpec((1, rows, heads * GROUP * HEAD_SIZE), lambda i: (0, 0, i))
    key_block = pl.BlockSpec((Y, rows, span), lambda i: (0, 0, i))
    value_block = pl.BlockSpec((Y, rows, span), lambda i: (0, 0, i + steps))
    place_block = pl.BlockSpec((Y, rows, 128), lambda i: (0, 0, 2 * KEY_VALUE_HEADS))

    def whole(*shape):
        return pl.BlockSpec(shape, lambda i: (0,) * len(shape))

    along = pl.pallas_call(
        forward_kernel,
        out_shape=jax.ShapeDtypeStruct((rows, 128), jnp.float32),
        compiler_params=params(),
        cost_estimate=pl.CostEstimate(
            flops=4 * rows * width * Y * rows,
            bytes_accessed=6 * rows * width,
            transcendentals=rows * QUERY_HEADS * Y * rows,
        ),
        name="forward",
    )(chosen_query_rows, output_gradient, gathered, query_places)
    chunk = width // PLANE
    term = pl.pallas_call(
        router_kernel,
        out_shape=jax.ShapeDtypeStruct((PLANE, 1, chunk), jnp.float32),
        compiler_params=params(),
        cost_estimate=pl.CostEstimate(
            flops=2 * rows * width, bytes_accessed=2 * rows * width, transcendentals=0
        ),
        name="router",
    )(along, slope, hidden_rows)

    query_gradient, *terms = pl.pallas_call(
        functools.partial(backward_kernel, heads),
        grid=(steps,),
        out_shape=[
            jax.ShapeDtypeStruct((1, rows, width), jnp.bfloat16),
            *[jax.ShapeDtypeStruct((rows, 2 * KV_WIDTH), jnp.bfloat16)] * Y,
        ],
        in_specs=[
            wide_block,
            wide_block,
            key_block,
            value_block,
            place_block,
            whole(1, GROUP * rows),
            whole(rows, 128),
        ],
        out_specs=[wide_block] + [pl.BlockSpec((rows, 2 * span), lambda i: (0, i))] * Y,
        compiler_params=params(FULL_VMEM),
        cost_estimate=pl.CostEstimate(
            flops=10 * rows * width * Y * rows,
            bytes_accessed=6 * rows * width,
            transcendentals=rows * QUERY_HEADS * Y * rows,
        ),
        name="backward",
    )(
        chosen_query_rows,
        output_gradient,
        gathered,
        gathered,
        gathered,
        query_places,
        gate,
    )

    plane = ("x", "core", "ctx")
    shares = lax.all_to_all(term, plane, 0, 0, tiled=True)
    share = fold(shares, Z, 8192)
    share, *terms = lax.optimization_barrier((share, *terms))
    lines = lax.all_to_all(share, "z", 0, 0, tiled=True)
    term_shares = [terms[0]] + [
        lax.ppermute(terms[back], "ctx", [(i, (i - back) % Y) for i in range(Y)])
        for back in range(1, Y)
    ]
    line = fold(lines, PLANE, FOLD_FLOPS)
    router_grad = lax.all_to_all(line, plane, 0, 0, tiled=True).reshape(width)
    key_gradient, value_gradient = pl.pallas_call(
        functools.partial(combine_kernel, span),
        out_shape=[jax.ShapeDtypeStruct((1, rows, KV_WIDTH), jnp.bfloat16)] * 2,
        compiler_params=params(),
        cost_estimate=pl.CostEstimate(
            flops=4 * rows * KV_WIDTH, bytes_accessed=20 * rows * KV_WIDTH, transcendentals=0
        ),
        name="combine",
    )(*term_shares)
    return query_gradient, key_gradient, value_gradient, router_grad


def solution(mesh):
    fine = Mesh(mesh.devices.reshape(X, Z, CORES, Y), ("x", "z", "core", "ctx"))
    seq = ("x", "z", "core")
    rows3 = P(seq, "ctx", None)
    rows2 = P(seq, "ctx")
    return jax.shard_map(
        body,
        mesh=fine,
        in_specs=(rows3, rows3, rows3, rows3, rows3, rows2, rows2, P()),
        out_specs=(rows3, rows3, rows3, P()),
        check_vma=False,
    )
```

time: 110 us -> 85.8 us (0.78); the launches traced: 108 us -> 85.3 us
  blocking collectives: 57.5 us -> 15.8 us
  starting transfers between devices: 13.9 us -> 41.3 us
  local copies, waits for them, and re-layouts: 7.84 us -> 1.95 us
  waiting for transfers between devices: 14.5 us -> 9.01 us
  Pallas kernels: 11.3 us -> 15.8 us
  other arithmetic: 1.58 us -> 0 us
    all_to_all x3 -> x1, blocking collectives: 57.5 us -> 15.8 us  [body(): router_grad = lax.all_to_all(line, plane, 0, 0, tiled=True).reshape(width)]
    all_to_all x2, starting transfers between devices: 8.79 us -> 26.6 us  [the longest x1 14.9 us: body(): lines = lax.all_to_all(share, 'z', 0, 0, tiled=True)]
    ppermute x0 -> x3, starting transfers between devices: none -> 9.6 us  [body(): lax.ppermute(terms[back], 'ctx', [(i, (i - back) % Y) for i in range(Y)])]
    unnamed x23 -> x17, local copies, waits for them, and re-layouts: 7.12 us -> 1.88 us
    all_to_all x2, waiting for transfers between devices: 6.64 us -> 1.76 us  [the longest x1 1.75 us: body(): lines = lax.all_to_all(share, 'z', 0, 0, tiled=True)]
    pallas_call x1, Pallas kernels: 0.3 us -> 2.17 us  [body(): pl.pallas_call(gate_kernel, out_shape=[jax.ShapeDtypeStruct((rows, 128),...]
    reduce_sum x4 -> x0, other arithmetic: 1.58 us -> none  [the longest x1 0.75 us: body(): jnp.sum(key_shares.astype(jnp.float32), axis=0, keepdims=True)]
    pallas_call x1 -> x5, Pallas kernels: 3.28 us -> 4.3 us  [the longest x1 1.94 us: body(): pl.pallas_call(forward_kernel, out_shape=jax.ShapeDtypeStruct((rows, 128)...]
  transfers between devices with their start and end apart: 3 -> 6, of which waited for: 2 -> 2; matrix products, arithmetic and copies ran while one was open for 1% -> 0% of each run, Pallas kernels for 6% -> 11%
where the time goes in v2:
time: 85.8 us; the launch traced here: 85.3 us
  starting transfers between devices  41.3 us (48%)
  Pallas kernels  15.8 us (18%)
  blocking collectives  15.8 us (18%)
  waiting for transfers between devices  9.01 us (11%)
  local copies, waits for them, and re-layouts  1.95 us (2%)
  between operations  1.42 us (2%)
    all_to_all x1, blocking collectives, body(): router_grad = lax.all_to_all(line, plane, 0, 0, tiled=True).reshape(width)  15.8 us
    all_to_all x1, starting transfers between devices, body(): lines = lax.all_to_all(share, 'z', 0, 0, tiled=True)  14.9 us
    all_to_all x1, starting transfers between devices, body(): shares = lax.all_to_all(term, plane, 0, 0, tiled=True)  11.6 us
    ppermute x3, starting transfers between devices, body(): lax.ppermute(terms[back], 'ctx', [(i, (i - back) % Y) for i in range(Y)])  9.6 us
    all_to_all x1, waiting for transfers between devices, body(): gathered = lax.all_to_all(payload, 'ctx', 0, 0, tiled=True)  7.25 us
    pallas_call x1, Pallas kernels, body(): pl.pallas_call(functools.partial(backward_kernel, heads), grid=(steps,),...  7.25 us
    all_to_all x1, starting transfers between devices, body(): gathered = lax.all_to_all(payload, 'ctx', 0, 0, tiled=True)  5.16 us
    pallas_call x1, Pallas kernels, body(): pl.pallas_call(gate_kernel, out_shape=[jax.ShapeDtypeStruct((rows, 128),...  2.17 us
  transfers between devices with their start and end apart: 6, of which 2 were waited for; matrix products, arithmetic and copies ran while one was open for 0% of the time, Pallas kernels for 11%

profile of v2, /device:TPU:1, one launch (start us, length us, event | category | flops | bytes accessed | tf_op | source)
XLA Modules:
  0.0 85.3 jit_solution(13310899886481488257)
XLA Ops:
  0.6 2.1 %pack.1 = bf16[4,64,2176]{2,1,0:T(8,128)(2,1)} custom-call(bf16[1,64,1024]{2,1,0:T(8,128)(2,1)} %key_ref.1, bf16[1,64,1024]{2,1,0:T(8,128)(2,1)} %value_ref.1, s32[1,64]{1,0:T(1,128)} %place_ref.1), custom_call_target="tpu_custom_call" | custom-call | tf_op jit(solution)/shard_map/pack/pallas_call | solution.py:250
  2.7 0.0 copy-start.7
  2.7 0.0 copy-start.2
  2.7 5.2 %all-to-all-start = ((bf16[4,64,2176]{2,1,0:T(8,128)(2,1)}), bf16[4,64,2176]{2,1,0:T(8,128)(2,1)S(1)}, u32[]{:S(2)}, u32[]{:S(2)}) async-start(bf16[4,64,2176]{2,1,0:T(8,128)(2,1)} %pack.1), calls=%async_computation | async-start | bytes 2228224 | tf_op jit(solution)/shard_map/all_to_all | solution.py:264
  8.5 0.0 copy-done.7
  8.6 0.1 tile.13.qp_ref
  8.6 0.0 copy-start.6
  8.6 2.2 %gate.1 = (f32[64,128]{1,0:T(8,128)}, f32[64,128]{1,0:T(8,128)}) custom-call(bf16[1,64,8192]{2,1,0:T(8,128)(2,1)} %hidden_ref.3, f32[1,8192]{1,0:T(1,128)} %bitcast.4, s32[1,1]{1,0:T(1,128)S(6)} %copy.13.count_ref), custom_call_target="tpu_custom_call" | custom-call | flops 1048576 | bytes 1048576 | tf_op jit(solution)/shard_map/gate/pallas_call | solution.py:266
  10.8 0.0 copy-start.1
  10.8 7.2 %all-to-all-done.k_ref.v_ref.kp_ref.pay_ref = bf16[4,64,2176]{2,1,0:T(8,128)(2,1)S(1)} async-done(((bf16[4,64,2176]{2,1,0:T(8,128)(2,1)}), bf16[4,64,2176]{2,1,0:T(8,128)(2,1)S(1)}, u32[]{:S(2)}, u32[]{:S(2)}) %all-to-all-start) | async-done | bytes 1114144 | tf_op jit(solution)/shard_map/all_to_all | solution.py:264
  18.1 0.0 copy-done.2
  18.1 0.0 copy-start.3
  18.1 1.2 %copy-done.3 = bf16[1,64,8192]{2,1,0:T(8,128)(2,1)S(1)} copy-done((bf16[1,64,8192]{2,1,0:T(8,128)(2,1)S(1)}, bf16[1,64,8192]{2,1,0:T(8,128)(2,1)}, u32[]{:S(2)}) %copy-start.3) | copy-done | bytes 1048600
  19.3 0.0 copy-start
  19.3 0.0 copy-start.5
  19.3 1.9 %forward.1.along_ref = f32[64,128]{1,0:T(8,128)S(1)} custom-call(bf16[1,64,8192]{2,1,0:T(8,128)(2,1)S(1)} %copy-done.2, bf16[1,64,8192]{2,1,0:T(8,128)(2,1)S(1)} %copy-done.3, bf16[4,64,2176]{2,1,0:T(8,128)(2,1)S(1)} %all-to-all-done.k_ref.v_ref.kp_ref.pay_ref, s32[1,512]{1,0:T(1,128)S(1)} %tile.13.qp_ref), custom_call_target="tpu_custom_call" | custom-call | flops 536870912 | bytes 3145728 | tf_op jit(solution)/shard_map/forward/pallas_call | solution.py:293
  21.2 0.0 copy-done.6
  21.2 0.0 copy-done
  21.2 0.0 copy-done.1
  21.2 0.0 copy-done.5
  21.3 0.9 %router.1 = f32[32,1,256]{2,1,0:T(1,128)} custom-call(f32[64,128]{1,0:T(8,128)S(1)} %forward.1.along_ref, f32[64,128]{1,0:T(8,128)S(1)} %copy-done.5, bf16[1,64,8192]{2,1,0:T(8,128)(2,1)S(1)} %copy-done.1), custom_call_target="tpu_custom_call" | custom-call | flops 1048576 | bytes 1048576 | tf_op jit(solution)/shard_map/router/pallas_call | solution.py:305
  22.1 11.6 %all-to-all-start.1 = ((f32[32,1,256]{2,1,0:T(1,128)}), f32[32,1,256]{2,1,0:T(1,128)S(1)}, u32[]{:S(2)}, u32[]{:S(2)}) async-start(f32[32,1,256]{2,1,0:T(1,128)} %router.1), calls=%async_computation.1 | async-start | bytes 65536 | tf_op jit(solution)/shard_map/all_to_all | solution.py:350
  33.8 7.2 %backward.1 = (bf16[1,64,8192]{2,1,0:T(8,128)(2,1)}, bf16[64,2048]{1,0:T(8,128)(2,1)}, bf16[64,2048]{1,0:T(8,128)(2,1)}, bf16[64,2048]{1,0:T(8,128)(2,1)}, bf16[64,2048]{1,0:T(8,128)(2,1)}) custom-call(bf16[1,64,8192]{2,1,0:T(8,128)(2,1)} %q_ref.3, bf16[1,64,8192]{2,1,0:T(8,128)(2,1)} %grad_ref.3, bf16[4,64,2176]{2,1,0:T(8,128)(2,1)} %copy-done, ...), custom_call_target="tpu_custom_call" | custom-call | flops 1342177280 | bytes 3145728 | tf_op jit(solution)/shard_map/backward/pallas_call | solution.py:315
  41.0 0.0 all-to-all-done.1.share_ref
  41.0 0.6 fold.2
  41.7 14.9 %all-to-all-start.2 = ((f32[16,1,256]{2,1,0:T(1,128)}), f32[16,1,256]{2,1,0:T(1,128)S(1)}, u32[]{:S(2)}, u32[]{:S(2)}) async-start(f32[16,1,256]{2,1,0:T(1,128)} %fold.2), calls=%async_computation.2 | async-start | bytes 32768 | tf_op jit(solution)/shard_map/all_to_all | solution.py:353
  56.6 0.0 copy-start.4
  56.6 4.6 %collective-permute-start = (bf16[64,2048]{1,0:T(8,128)(2,1)}, bf16[64,2048]{1,0:T(8,128)(2,1)S(1)}, u32[]{:S(2)}, u32[]{:S(2)}) collective-permute-start(bf16[64,2048]{1,0:T(8,128)(2,1)} %get-tuple-element.26), channel_id=1, source_target_pairs={{0,3},{1,0},{2,1},{3,2},{4,7},{5,4},{6,5},{7,6},{8,11},{9,8},{10,9... | collective-permute-start | bytes 786440 | tf_op jit(solution)/shard_map/ppermute | solution.py:355
  61.3 2.5 %collective-permute-start.1 = (bf16[64,2048]{1,0:T(8,128)(2,1)}, bf16[64,2048]{1,0:T(8,128)(2,1)S(1)}, u32[]{:S(2)}, u32[]{:S(2)}) collective-permute-start(bf16[64,2048]{1,0:T(8,128)(2,1)} %get-tuple-element.27), channel_id=1, source_target_pairs={{0,2},{1,3},{2,0},{3,1},{4,6},{5,7},{6,4},{7,5},{8,10},{9,11},{10,... | collective-permute-start | bytes 786440 | tf_op jit(solution)/shard_map/ppermute | solution.py:355
  63.7 2.5 %collective-permute-start.2 = (bf16[64,2048]{1,0:T(8,128)(2,1)}, bf16[64,2048]{1,0:T(8,128)(2,1)S(1)}, u32[]{:S(2)}, u32[]{:S(2)}) collective-permute-start(bf16[64,2048]{1,0:T(8,128)(2,1)} %get-tuple-element.28), channel_id=1, source_target_pairs={{0,1},{1,2},{2,3},{3,0},{4,5},{5,6},{6,7},{7,4},{8,9},{9,10},{10,1... | collective-permute-start | bytes 786440 | tf_op jit(solution)/shard_map/ppermute | solution.py:355
  66.2 1.8 %all-to-all-done.2.share_ref = f32[16,1,256]{2,1,0:T(1,128)S(1)} async-done(((f32[16,1,256]{2,1,0:T(1,128)}), f32[16,1,256]{2,1,0:T(1,128)S(1)}, u32[]{:S(2)}, u32[]{:S(2)}) %all-to-all-start.2) | async-done | bytes 16416 | tf_op jit(solution)/shard_map/all_to_all | solution.py:353
  68.0 15.8 %all_to_all.20 = f32[32,1,256]{2,1,0:T(1,128)S(1)} all-to-all(f32[32,1,256]{2,1,0:T(1,128)S(1)} %fold.3), channel_id=1, replica_groups=mesh['x'=4,'z'=16,'core'=2,'ctx'=4] {'x','core','ctx'}, dimensions={0} | all-to-all | bytes 65536 | tf_op jit(solution)/shard_map/all_to_all | solution.py:359
  83.8 0.0 collective-permute-done.refs_1_
  83.8 0.0 collective-permute-done.1.refs_2_
  83.8 0.0 collective-permute-done.2.refs_3_
  83.8 0.0 copy-done.4
  83.8 0.8 combine.1
  84.7 0.6 copy.14
  (2 shorter events, 0.0 us)
Async XLA Ops:
  2.7 5.8 %copy-start.7 = (s32[1,64]{1,0:T(1,128)S(1)}, s32[1,64]{1,0:T(1,128)}, u32[]{:S(2)}) copy-start(s32[1,64]{1,0:T(1,128)} %place_ref.1) | copy-start | bytes 772
  2.7 15.3 %copy-start.2 = (bf16[1,64,8192]{2,1,0:T(8,128)(2,1)S(1)}, bf16[1,64,8192]{2,1,0:T(8,128)(2,1)}, u32[]{:S(2)}) copy-start(bf16[1,64,8192]{2,1,0:T(8,128)(2,1)} %q_ref.3) | copy-start | bytes 3145732
  2.7 15.3 %all-to-all-start = ((bf16[4,64,2176]{2,1,0:T(8,128)(2,1)}), bf16[4,64,2176]{2,1,0:T(8,128)(2,1)S(1)}, u32[]{:S(2)}, u32[]{:S(2)}) async-start(bf16[4,64,2176]{2,1,0:T(8,128)(2,1)} %pack.1), calls=%async_computation | async-start | bytes 2228224 | tf_op jit(solution)/shard_map/all_to_all | solution.py:264
  8.6 12.6 %copy-start.6 = (s32[1,512]{1,0:T(1,128)}, s32[1,512]{1,0:T(1,128)S(1)}, u32[]{:S(2)}) copy-start(s32[1,512]{1,0:T(1,128)S(1)} %tile.13.qp_ref) | copy-start | bytes 6148
  10.8 10.4 %copy-start.1 = (bf16[1,64,8192]{2,1,0:T(8,128)(2,1)S(1)}, bf16[1,64,8192]{2,1,0:T(8,128)(2,1)}, u32[]{:S(2)}) copy-start(bf16[1,64,8192]{2,1,0:T(8,128)(2,1)} %hidden_ref.3) | copy-start | bytes 3145732
  18.1 1.2 %copy-start.3 = (bf16[1,64,8192]{2,1,0:T(8,128)(2,1)S(1)}, bf16[1,64,8192]{2,1,0:T(8,128)(2,1)}, u32[]{:S(2)}) copy-start(bf16[1,64,8192]{2,1,0:T(8,128)(2,1)} %grad_ref.3) | copy-start | bytes 3145732
  19.3 1.9 %copy-start = (bf16[4,64,2176]{2,1,0:T(8,128)(2,1)}, bf16[4,64,2176]{2,1,0:T(8,128)(2,1)S(1)}, u32[]{:S(2)}) copy-start(bf16[4,64,2176]{2,1,0:T(8,128)(2,1)S(1)} %all-to-all-done.k_ref.v_ref.kp_ref.pay_ref) | copy-start | bytes 3342340
  19.3 2.0 %copy-start.5 = (f32[64,128]{1,0:T(8,128)S(1)}, f32[64,128]{1,0:T(8,128)}, u32[]{:S(2)}) copy-start(f32[64,128]{1,0:T(8,128)} %get-tuple-element.20.slope_ref) | copy-start | bytes 98308
  22.1 18.9 %all-to-all-start.1 = ((f32[32,1,256]{2,1,0:T(1,128)}), f32[32,1,256]{2,1,0:T(1,128)S(1)}, u32[]{:S(2)}, u32[]{:S(2)}) async-start(f32[32,1,256]{2,1,0:T(1,128)} %router.1), calls=%async_computation.1 | async-start | bytes 65536 | tf_op jit(solution)/shard_map/all_to_all | solution.py:350
  41.7 26.3 %all-to-all-start.2 = ((f32[16,1,256]{2,1,0:T(1,128)}), f32[16,1,256]{2,1,0:T(1,128)S(1)}, u32[]{:S(2)}, u32[]{:S(2)}) async-start(f32[16,1,256]{2,1,0:T(1,128)} %fold.2), calls=%async_computation.2 | async-start | bytes 32768 | tf_op jit(solution)/shard_map/all_to_all | solution.py:353
  56.6 27.2 %copy-start.4 = (bf16[64,2048]{1,0:T(8,128)(2,1)S(1)}, bf16[64,2048]{1,0:T(8,128)(2,1)}, u32[]{:S(2)}) copy-start(bf16[64,2048]{1,0:T(8,128)(2,1)} %get-tuple-element.25.refs_0_) | copy-start | bytes 786436
  56.6 27.2 %collective-permute-start = (bf16[64,2048]{1,0:T(8,128)(2,1)}, bf16[64,2048]{1,0:T(8,128)(2,1)S(1)}, u32[]{:S(2)}, u32[]{:S(2)}) collective-permute-start(bf16[64,2048]{1,0:T(8,128)(2,1)} %get-tuple-element.26), channel_id=1, source_target_pairs={{0,3},{1,0},{2,1},{3,2},{4,7},{5,4},{6,5},{7,6},{8,11},{9,8},{10,9... | collective-permute-start | bytes 786440 | tf_op jit(solution)/shard_map/ppermute | solution.py:355
  61.3 22.6 %collective-permute-start.1 = (bf16[64,2048]{1,0:T(8,128)(2,1)}, bf16[64,2048]{1,0:T(8,128)(2,1)S(1)}, u32[]{:S(2)}, u32[]{:S(2)}) collective-permute-start(bf16[64,2048]{1,0:T(8,128)(2,1)} %get-tuple-element.27), channel_id=1, source_target_pairs={{0,2},{1,3},{2,0},{3,1},{4,6},{5,7},{6,4},{7,5},{8,10},{9,11},{10,... | collective-permute-start | bytes 786440 | tf_op jit(solution)/shard_map/ppermute | solution.py:355
  63.7 20.1 %collective-permute-start.2 = (bf16[64,2048]{1,0:T(8,128)(2,1)}, bf16[64,2048]{1,0:T(8,128)(2,1)S(1)}, u32[]{:S(2)}, u32[]{:S(2)}) collective-permute-start(bf16[64,2048]{1,0:T(8,128)(2,1)} %get-tuple-element.28), channel_id=1, source_target_pairs={{0,1},{1,2},{2,3},{3,0},{4,5},{5,6},{6,7},{7,4},{8,9},{9,10},{10,1... | collective-permute-start | bytes 786440 | tf_op jit(solution)/shard_map/ppermute | solution.py:355

commit v3 on v2

--- a/solution.py
+++ b/solution.py
@@ -17,8 +17,10 @@
 LOG2_SCALE = SCALE * math.log2(math.e)
 X, Z, CORES, Y = 4, 16, 2, 4
 PLANE = X * CORES * Y
+Y_FIRST, Z_FIRST, PLANE_FIRST = 0, 10, 17
 VMEM_LIMIT = 48 * 1024 * 1024
 FULL_VMEM = 60 * 1024 * 1024
+FORWARD_VMEM = 50 * 1024 * 1024
 FOLD_FLOPS = 1 << 35
 HBM = pl.BlockSpec(memory_space=pltpu.HBM)
 NT = (((1,), (1,)), ((), ()))
@@ -28,6 +30,12 @@
 
 def dot(a, b, dims):
     return lax.dot_general(a, b, dims, preferred_element_type=jnp.float32)
+
+
+def exchange(parts, axis, first):
+    size = parts.shape[0]
+    order = [(i + first) % size for i in range(size)]
+    return lax.all_to_all(parts, axis, 0, 0, axis_index_groups=[order], tiled=True)
 
 
 def params(limit=VMEM_LIMIT):
@@ -105,27 +113,30 @@
     return jnp.where(places <= query_places.astype(jnp.float32), 0.0, -1e30)
 
 
-def weights_of(keys, queries, bias):
-    copies = GROUP * 64 // bias.shape[1]
-    scores = dot(keys, queries, NT) + jnp.concatenate([bias] * copies, axis=1)
+def weights_of(scores, bias):
+    scores = scores + jnp.concatenate([bias] * (scores.shape[1] // bias.shape[1]), axis=1)
     top = jnp.max(scores, axis=0, keepdims=True)
     weights = jnp.exp2((scores - top) * LOG2_SCALE)
     return weights, jnp.sum(weights, axis=0, keepdims=True)
 
 
-def forward_kernel(q_ref, grad_ref, pay_ref, qp_ref, out_ref):
+def forward_kernel(q_ref, grad_ref, pay_ref, qp_ref, slope_ref, hidden_ref, out_ref):
     rows = q_ref.shape[1]
     bias = mask_bias(key_places(pay_ref[:, :, 2 * KV_WIDTH :]), qp_ref[:, : 2 * rows])
-    acc = jnp.zeros((1, GROUP * rows), jnp.float32)
-    for c in range(KEY_VALUE_HEADS):
+
+    def products(c):
         left = c * HEAD_SIZE
         queries = stack_heads(q_ref[0], c * GROUP, rows)
         grads = stack_heads(grad_ref[0], c * GROUP, rows)
         keys = pay_ref[:, :, left : left + HEAD_SIZE].reshape(-1, HEAD_SIZE)
         left = left + KV_WIDTH
         values = pay_ref[:, :, left : left + HEAD_SIZE].reshape(-1, HEAD_SIZE)
-        weights, total = weights_of(keys, queries, bias)
-        along = dot(values, grads, NT)
+        return dot(keys, queries, NT), dot(values, grads, NT)
+
+    acc = jnp.zeros((1, GROUP * rows), jnp.float32)
+    for c in range(KEY_VALUE_HEADS):
+        scores, along = products(c)
+        weights, total = weights_of(scores, bias)
         acc = acc + jnp.sum(weights * along, axis=0, keepdims=True) / total
     row_sum = acc[:, :rows]
     for g in range(1, GROUP):
@@ -135,12 +146,8 @@
         jnp.int32, (rows, rows), 1
     )
     down = jnp.sum(jnp.where(diagonal, wide, 0.0), axis=1, keepdims=True)
-    out_ref[...] = jnp.broadcast_to(down, (rows, 128))
-
-
-def router_kernel(along_ref, slope_ref, hidden_ref, out_ref):
-    rows, chunk = hidden_ref.shape[1], out_ref.shape[2]
-    logit_grad = along_ref[...] * slope_ref[...] * (1.0 / math.sqrt(X * Z * CORES * Y * rows))
+    logit_grad = down * slope_ref[...] * (1.0 / math.sqrt(X * Z * CORES * Y * rows))
+    chunk = out_ref.shape[2]
     for part in range(PLANE):
         for lane in range(0, chunk, 128):
             left = part * chunk + lane
@@ -164,7 +171,7 @@
 ):
     rows = q_ref.shape[1]
     me = lax.axis_index("ctx")
-    owners = [lax.rem(me + Y - back, Y) for back in range(Y)]
+    owners = [lax.rem(me + 2 * Y - back - Y_FIRST, Y) for back in range(Y)]
 
     def blocks(ref, columns):
         return jnp.concatenate([ref[owner, :, columns] for owner in owners], axis=0)
@@ -189,7 +196,7 @@
         beside = slice((heads + c) * HEAD_SIZE, (heads + c + 1) * HEAD_SIZE)
         keys = blocks(k_ref, own)
         values = blocks(v_ref, own)
-        weights, total = weights_of(keys, queries, bias)
+        weights, total = weights_of(dot(keys, queries, NT), bias)
         probs = (weights * (1.0 / total)).astype(jnp.bfloat16)
         probs32 = probs.astype(jnp.float32)
         grad_probs = dot(values, grads, NT)
@@ -261,7 +268,7 @@
         compiler_params=params(FULL_VMEM),
         name="pack",
     )(key_rows, chosen_value_rows, positions)
-    gathered = lax.all_to_all(payload, "ctx", 0, 0, tiled=True)
+    gathered = exchange(payload, "ctx", Y_FIRST)
 
     gate, slope = pl.pallas_call(
         gate_kernel,
@@ -271,7 +278,7 @@
             pl.BlockSpec(memory_space=pltpu.VMEM),
             pl.BlockSpec(memory_space=pltpu.SMEM),
         ],
-        compiler_params=params(FULL_VMEM),
+        compiler_params=params(FORWARD_VMEM),
         cost_estimate=pl.CostEstimate(
             flops=2 * rows * width, bytes_accessed=2 * rows * width, transcendentals=rows
         ),
@@ -290,27 +297,18 @@
     def whole(*shape):
         return pl.BlockSpec(shape, lambda i: (0,) * len(shape))
 
-    along = pl.pallas_call(
+    chunk = width // PLANE
+    term = pl.pallas_call(
         forward_kernel,
-        out_shape=jax.ShapeDtypeStruct((rows, 128), jnp.float32),
-        compiler_params=params(),
+        out_shape=jax.ShapeDtypeStruct((PLANE, 1, chunk), jnp.float32),
+        compiler_params=params(FORWARD_VMEM),
         cost_estimate=pl.CostEstimate(
             flops=4 * rows * width * Y * rows,
             bytes_accessed=6 * rows * width,
             transcendentals=rows * QUERY_HEADS * Y * rows,
         ),
         name="forward",
-    )(chosen_query_rows, output_gradient, gathered, query_places)
-    chunk = width // PLANE
-    term = pl.pallas_call(
-        router_kernel,
-        out_shape=jax.ShapeDtypeStruct((PLANE, 1, chunk), jnp.float32),
-        compiler_params=params(),
-        cost_estimate=pl.CostEstimate(
-            flops=2 * rows * width, bytes_accessed=2 * rows * width, transcendentals=0
-        ),
-        name="router",
-    )(along, slope, hidden_rows)
+    )(chosen_query_rows, output_gradient, gathered, query_places, slope, hidden_rows)
 
     query_gradient, *terms = pl.pallas_call(
         functools.partial(backward_kernel, heads),
@@ -347,16 +345,16 @@
     )
 
     plane = ("x", "core", "ctx")
-    shares = lax.all_to_all(term, plane, 0, 0, tiled=True)
+    shares = exchange(term, plane, PLANE_FIRST)
     share = fold(shares, Z, 8192)
     share, *terms = lax.optimization_barrier((share, *terms))
-    lines = lax.all_to_all(share, "z", 0, 0, tiled=True)
+    lines = exchange(share, "z", Z_FIRST)
     term_shares = [terms[0]] + [
         lax.ppermute(terms[back], "ctx", [(i, (i - back) % Y) for i in range(Y)])
         for back in range(1, Y)
     ]
     line = fold(lines, PLANE, FOLD_FLOPS)
-    router_grad = lax.all_to_all(line, plane, 0, 0, tiled=True).reshape(width)
+    router_grad = exchange(line, plane, PLANE_FIRST).reshape(width)
     key_gradient, value_gradient = pl.pallas_call(
         functools.partial(combine_kernel, span),
         out_shape=[jax.ShapeDtypeStruct((1, rows, KV_WIDTH), jnp.bfloat16)] * 2,
@@ -366,6 +364,7 @@
         ),
         name="combine",
     )(*term_shares)
+    router_grad, key_gradient = lax.optimization_barrier((router_grad, key_gradient))
     return query_gradient, key_gradient, value_gradient, router_grad
 
 

time: 85.8 us -> 84 us (0.979)
  blocking collectives: 15.8 us -> 0 us
  starting transfers between devices: 41.3 us -> 51.8 us
  waiting for transfers between devices: 9.01 us -> 13 us
    all_to_all x1 -> x0, blocking collectives: 15.8 us -> none  [body(): router_grad = lax.all_to_all(line, plane, 0, 0, tiled=True).reshape(width)]
    all_to_all x3 -> x4, starting transfers between devices: 31.7 us -> 42.9 us  [exchange(): lax.all_to_all(parts, axis, 0, 0, axis_index_groups=[order], tiled=True)]
    ppermute x3, waiting for transfers between devices: 0.01 us -> 4.45 us  [body(): lax.ppermute(terms[back], 'ctx', [(i, (i - back) % Y) for i in range(Y)])]
    pallas_call x1, Pallas kernels: 2.17 us -> 0.31 us  [body(): pl.pallas_call(gate_kernel, out_shape=[jax.ShapeDtypeStruct((rows, 128),...]
    pallas_call x2 -> x1, Pallas kernels: 2.81 us -> 4.18 us  [body(): pl.pallas_call(forward_kernel, out_shape=jax.ShapeDtypeStruct((PLANE, 1,...]
    all_to_all x3 -> x4, waiting for transfers between devices: 9.01 us -> 8.51 us  [exchange(): lax.all_to_all(parts, axis, 0, 0, axis_index_groups=[order], tiled=True)]
  transfers between devices with their start and end apart: 6 -> 7, of which waited for: 2 -> 2; matrix products, arithmetic and copies ran while one was open for 0% -> 0% of each run, Pallas kernels for 11% -> 11%
where the time goes in v3:
time: 84 us; the launch traced here: 83.5 us
  starting transfers between devices  51.8 us (62%)
  Pallas kernels  15.9 us (19%)
  waiting for transfers between devices  13 us (15%)
  between operations  1.44 us (2%)
  local copies, waits for them, and re-layouts  1.37 us (2%)
    all_to_all x4, starting transfers between devices, exchange(): lax.all_to_all(parts, axis, 0, 0, axis_index_groups=[order], tiled=True)  42.9 us
    ppermute x3, starting transfers between devices, body(): lax.ppermute(terms[back], 'ctx', [(i, (i - back) % Y) for i in range(Y)])  8.86 us
    all_to_all x4, waiting for transfers between devices, exchange(): lax.all_to_all(parts, axis, 0, 0, axis_index_groups=[order], tiled=True)  8.51 us
    pallas_call x1, Pallas kernels, body(): pl.pallas_call(functools.partial(backward_kernel, heads), grid=(steps,),...  7.25 us
    ppermute x3, waiting for transfers between devices, body(): lax.ppermute(terms[back], 'ctx', [(i, (i - back) % Y) for i in range(Y)])  4.45 us
    pallas_call x1, Pallas kernels, body(): pl.pallas_call(forward_kernel, out_shape=jax.ShapeDtypeStruct((PLANE, 1,...  4.18 us
    pallas_call x1, Pallas kernels, body(): pl.pallas_call(pack_kernel, out_shape=jax.ShapeDtypeStruct((Y, rows, 2 *...  2.12 us
  transfers between devices with their start and end apart: 7, of which 2 were waited for; matrix products, arithmetic and copies ran while one was open for 0% of the time, Pallas kernels for 11%

profile of v3, /device:TPU:1, one launch (start us, length us, event | category | flops | bytes accessed | tf_op | source)
XLA Modules:
  0.0 83.5 jit_solution(9594783347542250214)
XLA Ops:
  0.6 0.0 copy-start.2
  0.6 2.1 %pack.1 = bf16[4,64,2176]{2,1,0:T(8,128)(2,1)} custom-call(bf16[1,64,1024]{2,1,0:T(8,128)(2,1)} %key_ref.1, bf16[1,64,1024]{2,1,0:T(8,128)(2,1)} %value_ref.1, s32[1,64]{1,0:T(1,128)} %place_ref.1), custom_call_target="tpu_custom_call" | custom-call | tf_op jit(solution)/shard_map/pack/pallas_call | solution.py:257
  2.8 0.0 copy-start.7
  2.8 0.0 copy-start.5
  2.8 0.0 copy-start
  2.8 0.0 copy-start.1
  2.8 5.2 %all-to-all-start = ((bf16[4,64,2176]{2,1,0:T(8,128)(2,1)}), bf16[4,64,2176]{2,1,0:T(8,128)(2,1)}, u32[]{:S(2)}, u32[]{:S(2)}) async-start(bf16[4,64,2176]{2,1,0:T(8,128)(2,1)} %pack.1), calls=%async_computation | async-start | bytes 2228224 | tf_op jit(solution)/shard_map/all_to_all | solution.py:38
  8.6 0.0 copy-done.7
  8.6 0.1 tile.13.qp_ref
  8.7 0.0 copy-start.6
  8.7 0.0 copy-done.2
  8.7 0.0 copy-done.5
  8.7 0.3 gate.1
  9.0 0.0 copy-start.4
  9.0 0.6 copy-done.4
  9.7 8.5 %all-to-all-done.k_ref.v_ref.kp_ref.pay_ref = bf16[4,64,2176]{2,1,0:T(8,128)(2,1)} async-done(((bf16[4,64,2176]{2,1,0:T(8,128)(2,1)}), bf16[4,64,2176]{2,1,0:T(8,128)(2,1)}, u32[]{:S(2)}, u32[]{:S(2)}) %all-to-all-start) | async-done | bytes 1114144 | tf_op jit(solution)/shard_map/all_to_all | solution.py:38
  18.2 0.0 copy-done
  18.2 0.0 copy-done.1
  18.2 4.2 %forward.1 = f32[32,1,256]{2,1,0:T(1,128)} custom-call(bf16[1,64,8192]{2,1,0:T(8,128)(2,1)S(1)} %copy-done, bf16[1,64,8192]{2,1,0:T(8,128)(2,1)S(1)} %copy-done.1, bf16[4,64,2176]{2,1,0:T(8,128)(2,1)} %all-to-all-done.k_ref.v_ref.kp_ref.pay_ref, s32[1,512]{1,0:T(1,128)S(1)} %tile.13.qp_ref, f32[64,128]{1,0:T(8,128)S(1)} %get-tuple-element.22.slope_ref, ...), custom_call_target="tpu_custom_call" | custom-call | flops 536870912 | bytes 3145728 | tf_op jit(solution)/shard_map/forward/pallas_call | solution.py:301
  22.4 0.0 copy-done.6
  22.4 13.1 %all-to-all-start.1 = ((f32[32,1,256]{2,1,0:T(1,128)}), f32[32,1,256]{2,1,0:T(1,128)S(1)}, u32[]{:S(2)}, u32[]{:S(2)}) async-start(f32[32,1,256]{2,1,0:T(1,128)} %forward.1), calls=%async_computation.1 | async-start | bytes 65536 | tf_op jit(solution)/shard_map/all_to_all | solution.py:38
  35.4 7.2 %backward.1 = (bf16[1,64,8192]{2,1,0:T(8,128)(2,1)}, bf16[64,2048]{1,0:T(8,128)(2,1)}, bf16[64,2048]{1,0:T(8,128)(2,1)}, bf16[64,2048]{1,0:T(8,128)(2,1)}, bf16[64,2048]{1,0:T(8,128)(2,1)}) custom-call(bf16[1,64,8192]{2,1,0:T(8,128)(2,1)} %q_ref.3, bf16[1,64,8192]{2,1,0:T(8,128)(2,1)} %grad_ref.3, ...), custom_call_target="tpu_custom_call" | custom-call | flops 1342177280 | bytes 3145728 | tf_op jit(solution)/shard_map/backward/pallas_call | solution.py:313
  42.7 0.0 all-to-all-done.1.share_ref
  42.7 0.6 fold.2
  43.3 16.5 %all-to-all-start.2 = ((f32[16,1,256]{2,1,0:T(1,128)}), f32[16,1,256]{2,1,0:T(1,128)S(1)}, u32[]{:S(2)}, u32[]{:S(2)}) async-start(f32[16,1,256]{2,1,0:T(1,128)} %fold.2), calls=%async_computation.2 | async-start | bytes 32768 | tf_op jit(solution)/shard_map/all_to_all | solution.py:38
  59.8 0.0 copy-start.3
  59.8 4.5 %collective-permute-start = (bf16[64,2048]{1,0:T(8,128)(2,1)}, bf16[64,2048]{1,0:T(8,128)(2,1)S(1)}, u32[]{:S(2)}, u32[]{:S(2)}) collective-permute-start(bf16[64,2048]{1,0:T(8,128)(2,1)} %get-tuple-element.29), channel_id=1, source_target_pairs={{0,3},{1,0},{2,1},{3,2},{4,7},{5,4},{6,5},{7,6},{8,11},{9,8},{10,9... | collective-permute-start | bytes 786440 | tf_op jit(solution)/shard_map/ppermute | solution.py:353
  64.3 1.9 %collective-permute-start.1 = (bf16[64,2048]{1,0:T(8,128)(2,1)}, bf16[64,2048]{1,0:T(8,128)(2,1)S(1)}, u32[]{:S(2)}, u32[]{:S(2)}) collective-permute-start(bf16[64,2048]{1,0:T(8,128)(2,1)} %get-tuple-element.30), channel_id=1, source_target_pairs={{0,2},{1,3},{2,0},{3,1},{4,6},{5,7},{6,4},{7,5},{8,10},{9,11},{10,... | collective-permute-start | bytes 786440 | tf_op jit(solution)/shard_map/ppermute | solution.py:353
  66.2 2.5 %collective-permute-start.2 = (bf16[64,2048]{1,0:T(8,128)(2,1)}, bf16[64,2048]{1,0:T(8,128)(2,1)S(1)}, u32[]{:S(2)}, u32[]{:S(2)}) collective-permute-start(bf16[64,2048]{1,0:T(8,128)(2,1)} %get-tuple-element.31), channel_id=1, source_target_pairs={{0,1},{1,2},{2,3},{3,0},{4,5},{5,6},{6,7},{7,4},{8,9},{9,10},{10,1... | collective-permute-start | bytes 786440 | tf_op jit(solution)/shard_map/ppermute | solution.py:353
  68.7 0.0 all-to-all-done.2.share_ref
  68.7 0.6 fold.3
  69.4 8.2 %all-to-all-start.3 = ((f32[32,1,256]{2,1,0:T(1,128)}), f32[32,1,256]{2,1,0:T(1,128)S(1)}, u32[]{:S(2)}, u32[]{:S(2)}) async-start(f32[32,1,256]{2,1,0:T(1,128)} %fold.3), calls=%async_computation.3 | async-start | bytes 65536 | tf_op jit(solution)/shard_map/all_to_all | solution.py:38
  77.6 0.0 collective-permute-done.refs_1_
  77.6 0.0 collective-permute-done.1.refs_2_
  77.6 4.4 %collective-permute-done.2.refs_3_ = bf16[64,2048]{1,0:T(8,128)(2,1)S(1)} collective-permute-done((bf16[64,2048]{1,0:T(8,128)(2,1)}, bf16[64,2048]{1,0:T(8,128)(2,1)S(1)}, u32[]{:S(2)}, u32[]{:S(2)}) %collective-permute-start.2) | collective-permute-done | bytes 262176 | tf_op jit(solution)/shard_map/ppermute | solution.py:353
  82.0 0.0 copy-done.3
  82.0 0.8 combine.1
  82.8 0.0 all-to-all-done.3
  82.8 0.6 copy.14
  (1 shorter events, 0.0 us)
Async XLA Ops:
  0.6 8.1 %copy-start.2 = (bf16[1,64,8192]{2,1,0:T(8,128)(2,1)S(1)}, bf16[1,64,8192]{2,1,0:T(8,128)(2,1)}, u32[]{:S(2)}) copy-start(bf16[1,64,8192]{2,1,0:T(8,128)(2,1)} %hidden_ref.3) | copy-start | bytes 3145732
  2.8 5.9 %copy-start.7 = (s32[1,64]{1,0:T(1,128)S(1)}, s32[1,64]{1,0:T(1,128)}, u32[]{:S(2)}) copy-start(s32[1,64]{1,0:T(1,128)} %place_ref.1) | copy-start | bytes 772
  2.8 5.9 %copy-start.5 = (f32[8192]{0:T(1024)S(1)}, f32[8192]{0:T(1024)}, u32[]{:S(2)}) copy-start(f32[8192]{0:T(1024)} %param.15) | copy-start | bytes 98308
  2.8 15.4 %copy-start = (bf16[1,64,8192]{2,1,0:T(8,128)(2,1)S(1)}, bf16[1,64,8192]{2,1,0:T(8,128)(2,1)}, u32[]{:S(2)}) copy-start(bf16[1,64,8192]{2,1,0:T(8,128)(2,1)} %q_ref.3) | copy-start | bytes 3145732
  2.8 15.4 %copy-start.1 = (bf16[1,64,8192]{2,1,0:T(8,128)(2,1)S(1)}, bf16[1,64,8192]{2,1,0:T(8,128)(2,1)}, u32[]{:S(2)}) copy-start(bf16[1,64,8192]{2,1,0:T(8,128)(2,1)} %grad_ref.3) | copy-start | bytes 3145732
  2.8 15.4 %all-to-all-start = ((bf16[4,64,2176]{2,1,0:T(8,128)(2,1)}), bf16[4,64,2176]{2,1,0:T(8,128)(2,1)}, u32[]{:S(2)}, u32[]{:S(2)}) async-start(bf16[4,64,2176]{2,1,0:T(8,128)(2,1)} %pack.1), calls=%async_computation | async-start | bytes 2228224 | tf_op jit(solution)/shard_map/all_to_all | solution.py:38
  8.7 13.6 %copy-start.6 = (s32[1,512]{1,0:T(1,128)}, s32[1,512]{1,0:T(1,128)S(1)}, u32[]{:S(2)}) copy-start(s32[1,512]{1,0:T(1,128)S(1)} %tile.13.qp_ref) | copy-start | bytes 6148
  9.0 0.6 copy-start.4
  22.4 20.3 %all-to-all-start.1 = ((f32[32,1,256]{2,1,0:T(1,128)}), f32[32,1,256]{2,1,0:T(1,128)S(1)}, u32[]{:S(2)}, u32[]{:S(2)}) async-start(f32[32,1,256]{2,1,0:T(1,128)} %forward.1), calls=%async_computation.1 | async-start | bytes 65536 | tf_op jit(solution)/shard_map/all_to_all | solution.py:38
  43.3 25.4 %all-to-all-start.2 = ((f32[16,1,256]{2,1,0:T(1,128)}), f32[16,1,256]{2,1,0:T(1,128)S(1)}, u32[]{:S(2)}, u32[]{:S(2)}) async-start(f32[16,1,256]{2,1,0:T(1,128)} %fold.2), calls=%async_computation.2 | async-start | bytes 32768 | tf_op jit(solution)/shard_map/all_to_all | solution.py:38
  59.8 22.2 %copy-start.3 = (bf16[64,2048]{1,0:T(8,128)(2,1)S(1)}, bf16[64,2048]{1,0:T(8,128)(2,1)}, u32[]{:S(2)}) copy-start(bf16[64,2048]{1,0:T(8,128)(2,1)} %get-tuple-element.28.refs_0_) | copy-start | bytes 786436
  59.8 17.7 %collective-permute-start = (bf16[64,2048]{1,0:T(8,128)(2,1)}, bf16[64,2048]{1,0:T(8,128)(2,1)S(1)}, u32[]{:S(2)}, u32[]{:S(2)}) collective-permute-start(bf16[64,2048]{1,0:T(8,128)(2,1)} %get-tuple-element.29), channel_id=1, source_target_pairs={{0,3},{1,0},{2,1},{3,2},{4,7},{5,4},{6,5},{7,6},{8,11},{9,8},{10,9... | collective-permute-start | bytes 786440 | tf_op jit(solution)/shard_map/ppermute | solution.py:353
  64.3 13.3 %collective-permute-start.1 = (bf16[64,2048]{1,0:T(8,128)(2,1)}, bf16[64,2048]{1,0:T(8,128)(2,1)S(1)}, u32[]{:S(2)}, u32[]{:S(2)}) collective-permute-start(bf16[64,2048]{1,0:T(8,128)(2,1)} %get-tuple-element.30), channel_id=1, source_target_pairs={{0,2},{1,3},{2,0},{3,1},{4,6},{5,7},{6,4},{7,5},{8,10},{9,11},{10,... | collective-permute-start | bytes 786440 | tf_op jit(solution)/shard_map/ppermute | solution.py:353
  66.2 15.8 %collective-permute-start.2 = (bf16[64,2048]{1,0:T(8,128)(2,1)}, bf16[64,2048]{1,0:T(8,128)(2,1)S(1)}, u32[]{:S(2)}, u32[]{:S(2)}) collective-permute-start(bf16[64,2048]{1,0:T(8,128)(2,1)} %get-tuple-element.31), channel_id=1, source_target_pairs={{0,1},{1,2},{2,3},{3,0},{4,5},{5,6},{6,7},{7,4},{8,9},{9,10},{10,1... | collective-permute-start | bytes 786440 | tf_op jit(solution)/shard_map/ppermute | solution.py:353
  69.4 13.5 %all-to-all-start.3 = ((f32[32,1,256]{2,1,0:T(1,128)}), f32[32,1,256]{2,1,0:T(1,128)S(1)}, u32[]{:S(2)}, u32[]{:S(2)}) async-start(f32[32,1,256]{2,1,0:T(1,128)} %fold.3), calls=%async_computation.3 | async-start | bytes 65536 | tf_op jit(solution)/shard_map/all_to_all | solution.py:38

commit v4 on v3

--- a/solution.py
+++ b/solution.py
@@ -20,7 +20,6 @@
 Y_FIRST, Z_FIRST, PLANE_FIRST = 0, 10, 17
 VMEM_LIMIT = 48 * 1024 * 1024
 FULL_VMEM = 60 * 1024 * 1024
-FORWARD_VMEM = 50 * 1024 * 1024
 FOLD_FLOPS = 1 << 35
 HBM = pl.BlockSpec(memory_space=pltpu.HBM)
 NT = (((1,), (1,)), ((), ()))
@@ -79,24 +78,6 @@
         copy.wait()
 
 
-def gate_kernel(hidden_ref, router_ref, count_ref, gate_ref, slope_ref):
-    rows, width = hidden_ref.shape[1:]
-    step = 1024
-    total = jnp.zeros((rows, 128), jnp.float32)
-    for start in range(0, width, step):
-        product = hidden_ref[0, :, start : start + step].astype(jnp.float32) * router_ref[
-            :, start : start + step
-        ]
-        for piece in range(0, step, 128):
-            total = total + product[:, piece : piece + 128]
-    logits = jnp.sum(total, axis=1, keepdims=True)
-    sigma = jax.nn.sigmoid(logits)
-    slot = lax.broadcasted_iota(jnp.int32, (rows, 1), 0)
-    valid = (slot < count_ref[0, 0]).astype(jnp.float32)
-    gate_ref[...] = jnp.broadcast_to(sigma * valid, (rows, 128))
-    slope_ref[...] = jnp.broadcast_to(sigma * (1.0 - sigma) * valid, (rows, 128))
-
-
 def key_places(place_block):
     coded = place_block.reshape(-1, 128).astype(jnp.float32)
     return coded[:, 0:1] * 16.0 + coded[:, 1:2]
@@ -120,23 +101,20 @@
     return weights, jnp.sum(weights, axis=0, keepdims=True)
 
 
-def forward_kernel(q_ref, grad_ref, pay_ref, qp_ref, slope_ref, hidden_ref, out_ref):
+def forward_kernel(q_ref, grad_ref, pay_ref, qp_ref, out_ref):
     rows = q_ref.shape[1]
     bias = mask_bias(key_places(pay_ref[:, :, 2 * KV_WIDTH :]), qp_ref[:, : 2 * rows])
 
-    def products(c):
+    acc = jnp.zeros((1, GROUP * rows), jnp.float32)
+    for c in range(KEY_VALUE_HEADS):
         left = c * HEAD_SIZE
         queries = stack_heads(q_ref[0], c * GROUP, rows)
+        keys = pay_ref[:, :, left : left + HEAD_SIZE].reshape(-1, HEAD_SIZE)
+        weights, total = weights_of(dot(keys, queries, NT), bias)
+        left = left + KV_WIDTH
         grads = stack_heads(grad_ref[0], c * GROUP, rows)
-        keys = pay_ref[:, :, left : left + HEAD_SIZE].reshape(-1, HEAD_SIZE)
-        left = left + KV_WIDTH
         values = pay_ref[:, :, left : left + HEAD_SIZE].reshape(-1, HEAD_SIZE)
-        return dot(keys, queries, NT), dot(values, grads, NT)
-
-    acc = jnp.zeros((1, GROUP * rows), jnp.float32)
-    for c in range(KEY_VALUE_HEADS):
-        scores, along = products(c)
-        weights, total = weights_of(scores, bias)
+        along = dot(values, grads, NT)
         acc = acc + jnp.sum(weights * along, axis=0, keepdims=True) / total
     row_sum = acc[:, :rows]
     for g in range(1, GROUP):
@@ -146,7 +124,21 @@
         jnp.int32, (rows, rows), 1
     )
     down = jnp.sum(jnp.where(diagonal, wide, 0.0), axis=1, keepdims=True)
-    logit_grad = down * slope_ref[...] * (1.0 / math.sqrt(X * Z * CORES * Y * rows))
+    out_ref[...] = jnp.broadcast_to(down, (rows, 128))
+
+
+def router_kernel(along_ref, hidden_ref, router_ref, count_ref, out_ref, gate_ref):
+    rows, width = hidden_ref.shape[1:]
+    total = jnp.zeros((rows, 128), jnp.float32)
+    for left in range(0, width, 128):
+        block = hidden_ref[0, :, left : left + 128].astype(jnp.float32)
+        total = total + block * router_ref[:, left : left + 128]
+    sigma = jax.nn.sigmoid(jnp.sum(total, axis=1, keepdims=True))
+    slot = lax.broadcasted_iota(jnp.int32, (rows, 1), 0)
+    valid = (slot < count_ref[0, 0]).astype(jnp.float32)
+    gate_ref[...] = jnp.broadcast_to(sigma * valid, (rows, 128))
+    slope = sigma * (1.0 - sigma) * valid
+    logit_grad = along_ref[...] * slope * (1.0 / math.sqrt(X * Z * CORES * Y * rows))
     chunk = out_ref.shape[2]
     for part in range(PLANE):
         for lane in range(0, chunk, 128):
@@ -270,21 +262,6 @@
     )(key_rows, chosen_value_rows, positions)
     gathered = exchange(payload, "ctx", Y_FIRST)
 
-    gate, slope = pl.pallas_call(
-        gate_kernel,
-        out_shape=[jax.ShapeDtypeStruct((rows, 128), jnp.float32)] * 2,
-        in_specs=[
-            pl.BlockSpec(memory_space=pltpu.VMEM),
-            pl.BlockSpec(memory_space=pltpu.VMEM),
-            pl.BlockSpec(memory_space=pltpu.SMEM),
-        ],
-        compiler_params=params(FORWARD_VMEM),
-        cost_estimate=pl.CostEstimate(
-            flops=2 * rows * width, bytes_accessed=2 * rows * width, transcendentals=rows
-        ),
-        name="gate",
-    )(hidden_rows, router.reshape(1, width), counts)
-
     query_places = jnp.tile(positions, (1, GROUP))
     heads = 2
     steps = KEY_VALUE_HEADS // heads
@@ -297,18 +274,32 @@
     def whole(*shape):
         return pl.BlockSpec(shape, lambda i: (0,) * len(shape))
 
-    chunk = width // PLANE
-    term = pl.pallas_call(
+    along = pl.pallas_call(
         forward_kernel,
-        out_shape=jax.ShapeDtypeStruct((PLANE, 1, chunk), jnp.float32),
-        compiler_params=params(FORWARD_VMEM),
+        out_shape=jax.ShapeDtypeStruct((rows, 128), jnp.float32),
+        compiler_params=params(),
         cost_estimate=pl.CostEstimate(
             flops=4 * rows * width * Y * rows,
             bytes_accessed=6 * rows * width,
             transcendentals=rows * QUERY_HEADS * Y * rows,
         ),
         name="forward",
-    )(chosen_query_rows, output_gradient, gathered, query_places, slope, hidden_rows)
+    )(chosen_query_rows, output_gradient, gathered, query_places)
+    chunk = width // PLANE
+    vmem = pl.BlockSpec(memory_space=pltpu.VMEM)
+    term, gate = pl.pallas_call(
+        router_kernel,
+        out_shape=[
+            jax.ShapeDtypeStruct((PLANE, 1, chunk), jnp.float32),
+            jax.ShapeDtypeStruct((rows, 128), jnp.float32),
+        ],
+        in_specs=[vmem, vmem, vmem, pl.BlockSpec(memory_space=pltpu.SMEM)],
+        compiler_params=params(),
+        cost_estimate=pl.CostEstimate(
+            flops=4 * rows * width, bytes_accessed=2 * rows * width, transcendentals=rows
+        ),
+        name="router",
+    )(along, hidden_rows, router.reshape(1, width), counts)
 
     query_gradient, *terms = pl.pallas_call(
         functools.partial(backward_kernel, heads),
@@ -350,7 +341,7 @@
     share, *terms = lax.optimization_barrier((share, *terms))
     lines = exchange(share, "z", Z_FIRST)
     term_shares = [terms[0]] + [
-        lax.ppermute(terms[back], "ctx", [(i, (i - back) % Y) for i in range(Y)])
+        lax.ppermute(terms[back], "ctx", [(i, i - back) for i in range(back, Y)])
         for back in range(1, Y)
     ]
     line = fold(lines, PLANE, FOLD_FLOPS)

time: 84 us -> 80.4 us (0.957)
  starting transfers between devices: 51.8 us -> 49.7 us
  Pallas kernels: 15.9 us -> 14.6 us
    ppermute x3, starting transfers between devices: 8.86 us -> 4.01 us  [body(): lax.ppermute(terms[back], 'ctx', [(i, i - back) for i in range(back, Y)])]
    all_to_all x4, starting transfers between devices: 42.9 us -> 45.7 us  [exchange(): lax.all_to_all(parts, axis, 0, 0, axis_index_groups=[order], tiled=True)]
    ppermute x3, waiting for transfers between devices: 4.45 us -> 2.99 us  [body(): lax.ppermute(terms[back], 'ctx', [(i, i - back) for i in range(back, Y)])]
    all_to_all x4, waiting for transfers between devices: 8.51 us -> 9.92 us  [exchange(): lax.all_to_all(parts, axis, 0, 0, axis_index_groups=[order], tiled=True)]
    pallas_call x2, Pallas kernels: 4.48 us -> 3.13 us  [the longest x1 1.94 us: body(): pl.pallas_call(forward_kernel, out_shape=jax.ShapeDtypeStruct((rows, 128)...]
  transfers between devices with their start and end apart: 7 -> 7, of which waited for: 2 -> 3; matrix products, arithmetic and copies ran while one was open for 0% -> 0% of each run, Pallas kernels for 11% -> 11%
where the time goes in v4:
time: 80.4 us; the launch traced here: 80 us
  starting transfers between devices  49.7 us (62%)
  Pallas kernels  14.6 us (18%)
  waiting for transfers between devices  12.9 us (16%)
  between operations  1.44 us (2%)
  local copies, waits for them, and re-layouts  1.35 us (2%)
    all_to_all x4, starting transfers between devices, exchange(): lax.all_to_all(parts, axis, 0, 0, axis_index_groups=[order], tiled=True)  45.7 us
    all_to_all x4, waiting for transfers between devices, exchange(): lax.all_to_all(parts, axis, 0, 0, axis_index_groups=[order], tiled=True)  9.92 us
    pallas_call x1, Pallas kernels, body(): pl.pallas_call(functools.partial(backward_kernel, heads), grid=(steps,),...  7.24 us
    ppermute x3, starting transfers between devices, body(): lax.ppermute(terms[back], 'ctx', [(i, i - back) for i in range(back, Y)])  4.01 us
    ppermute x3, waiting for transfers between devices, body(): lax.ppermute(terms[back], 'ctx', [(i, i - back) for i in range(back, Y)])  2.99 us
    pallas_call x1, Pallas kernels, body(): pl.pallas_call(pack_kernel, out_shape=jax.ShapeDtypeStruct((Y, rows, 2 *...  2.08 us
    pallas_call x1, Pallas kernels, body(): pl.pallas_call(forward_kernel, out_shape=jax.ShapeDtypeStruct((rows, 128)...  1.94 us
  transfers between devices with their start and end apart: 7, of which 3 were waited for; matrix products, arithmetic and copies ran while one was open for 0% of the time, Pallas kernels for 11%

profile of v4, /device:TPU:1, one launch (start us, length us, event | category | flops | bytes accessed | tf_op | source)
XLA Modules:
  0.0 80.0 jit_solution(34782804350192324)
XLA Ops:
  0.6 2.1 %pack.1 = bf16[4,64,2176]{2,1,0:T(8,128)(2,1)} custom-call(bf16[1,64,1024]{2,1,0:T(8,128)(2,1)} %key_ref.1, bf16[1,64,1024]{2,1,0:T(8,128)(2,1)} %value_ref.1, s32[1,64]{1,0:T(1,128)} %place_ref.1), custom_call_target="tpu_custom_call" | custom-call | tf_op jit(solution)/shard_map/pack/pallas_call | solution.py:249
  2.7 0.0 copy-start.8
  2.7 0.0 copy-start.1
  2.7 0.0 copy-start.2
  2.8 5.2 %all-to-all-start = ((bf16[4,64,2176]{2,1,0:T(8,128)(2,1)}), bf16[4,64,2176]{2,1,0:T(8,128)(2,1)S(1)}, u32[]{:S(2)}, u32[]{:S(2)}) async-start(bf16[4,64,2176]{2,1,0:T(8,128)(2,1)} %pack.1), calls=%async_computation | async-start | bytes 2228224 | tf_op jit(solution)/shard_map/all_to_all | solution.py:37
  8.6 0.0 copy-done.8
  8.6 0.1 tile.13.qp_ref
  8.7 0.0 copy-start.7
  8.7 0.0 copy-start.6
  8.7 9.4 %all-to-all-done.pay_ref.k_ref.v_ref.kp_ref = bf16[4,64,2176]{2,1,0:T(8,128)(2,1)S(1)} async-done(((bf16[4,64,2176]{2,1,0:T(8,128)(2,1)}), bf16[4,64,2176]{2,1,0:T(8,128)(2,1)S(1)}, u32[]{:S(2)}, u32[]{:S(2)}) %all-to-all-start) | async-done | bytes 1114144 | tf_op jit(solution)/shard_map/all_to_all | solution.py:37
  18.1 0.0 copy-done.1
  18.1 0.0 copy-done.2
  18.1 0.0 copy-start
  18.1 0.0 copy-start.3
  18.1 1.9 %forward.1.along_ref = f32[64,128]{1,0:T(8,128)S(1)} custom-call(bf16[1,64,8192]{2,1,0:T(8,128)(2,1)S(1)} %copy-done.1, bf16[1,64,8192]{2,1,0:T(8,128)(2,1)S(1)} %copy-done.2, bf16[4,64,2176]{2,1,0:T(8,128)(2,1)S(1)} %all-to-all-done.pay_ref.k_ref.v_ref.kp_ref, s32[1,512]{1,0:T(1,128)S(1)} %tile.13.qp_ref), custom_call_target="tpu_custom_call" | custom-call | flops 536870912 | bytes 3145728 | tf_op jit(solution)/shard_map/forward/pallas_call | solution.py:277
  20.1 0.0 copy-done.7
  20.1 0.0 copy-done
  20.1 0.0 copy-done.6
  20.1 0.0 copy-done.3
  20.1 1.2 %router.1 = (f32[32,1,256]{2,1,0:T(1,128)}, f32[64,128]{1,0:T(8,128)S(1)}) custom-call(f32[64,128]{1,0:T(8,128)S(1)} %forward.1.along_ref, bf16[1,64,8192]{2,1,0:T(8,128)(2,1)S(1)} %copy-done.3, f32[1,8192]{1,0:T(1,128)S(1)} %bitcast.3, s32[1,1]{1,0:T(1,128)S(6)} %copy.13.count_ref), custom_call_target="tpu_custom_call" | custom-call | flops 2097152 | bytes 1048576 | tf_op jit(solution)/shard_map/router/pallas_call | solution.py:290
  21.3 0.0 copy-start.5
  21.3 0.6 copy-done.5
  21.9 12.8 %all-to-all-start.1 = ((f32[32,1,256]{2,1,0:T(1,128)}), f32[32,1,256]{2,1,0:T(1,128)S(1)}, u32[]{:S(2)}, u32[]{:S(2)}) async-start(f32[32,1,256]{2,1,0:T(1,128)} %get-tuple-element.22), calls=%async_computation.1 | async-start | bytes 65536 | tf_op jit(solution)/shard_map/all_to_all | solution.py:37
  34.7 7.2 %backward.1 = (bf16[1,64,8192]{2,1,0:T(8,128)(2,1)}, bf16[64,2048]{1,0:T(8,128)(2,1)}, bf16[64,2048]{1,0:T(8,128)(2,1)}, bf16[64,2048]{1,0:T(8,128)(2,1)}, bf16[64,2048]{1,0:T(8,128)(2,1)}) custom-call(bf16[1,64,8192]{2,1,0:T(8,128)(2,1)} %q_ref.3, bf16[1,64,8192]{2,1,0:T(8,128)(2,1)} %grad_ref.3, bf16[4,64,2176]{2,1,0:T(8,128)(2,1)} %copy-done, ...), custom_call_target="tpu_custom_call" | custom-call | flops 1342177280 | bytes 3145728 | tf_op jit(solution)/shard_map/backward/pallas_call | solution.py:304
  42.0 0.0 all-to-all-done.1.share_ref
  42.0 0.6 fold.2
  42.6 16.5 %all-to-all-start.2 = ((f32[16,1,256]{2,1,0:T(1,128)}), f32[16,1,256]{2,1,0:T(1,128)S(1)}, u32[]{:S(2)}, u32[]{:S(2)}) async-start(f32[16,1,256]{2,1,0:T(1,128)} %fold.2), calls=%async_computation.2 | async-start | bytes 32768 | tf_op jit(solution)/shard_map/all_to_all | solution.py:37
  59.1 0.0 copy-start.4
  59.1 1.4 %collective-permute-start = (bf16[64,2048]{1,0:T(8,128)(2,1)}, bf16[64,2048]{1,0:T(8,128)(2,1)S(1)}, u32[]{:S(2)}, u32[]{:S(2)}) collective-permute-start(bf16[64,2048]{1,0:T(8,128)(2,1)} %get-tuple-element.29), channel_id=1, source_target_pairs={{1,0},{2,1},{3,2},{5,4},{6,5},{7,6},{9,8},{10,9},{11,10},{13,12},{... | collective-permute-start | bytes 786440 | tf_op jit(solution)/shard_map/ppermute | solution.py:344
  60.6 1.3 %collective-permute-start.1 = (bf16[64,2048]{1,0:T(8,128)(2,1)}, bf16[64,2048]{1,0:T(8,128)(2,1)S(1)}, u32[]{:S(2)}, u32[]{:S(2)}) collective-permute-start(bf16[64,2048]{1,0:T(8,128)(2,1)} %get-tuple-element.30), channel_id=1, source_target_pairs={{2,0},{3,1},{6,4},{7,5},{10,8},{11,9},{14,12},{15,13},{18,16},{19,... | collective-permute-start | bytes 786440 | tf_op jit(solution)/shard_map/ppermute | solution.py:344
  61.9 1.3 %collective-permute-start.2 = (bf16[64,2048]{1,0:T(8,128)(2,1)}, bf16[64,2048]{1,0:T(8,128)(2,1)S(1)}, u32[]{:S(2)}, u32[]{:S(2)}) collective-permute-start(bf16[64,2048]{1,0:T(8,128)(2,1)} %get-tuple-element.31), channel_id=1, source_target_pairs={{3,0},{7,4},{11,8},{15,12},{19,16},{23,20},{27,24},{31,28},{35,32}... | collective-permute-start | bytes 786440 | tf_op jit(solution)/shard_map/ppermute | solution.py:344
  63.2 0.0 all-to-all-done.2.share_ref
  63.2 0.6 fold.3
  63.8 11.2 %all-to-all-start.3 = ((f32[32,1,256]{2,1,0:T(1,128)}), f32[32,1,256]{2,1,0:T(1,128)S(1)}, u32[]{:S(2)}, u32[]{:S(2)}) async-start(f32[32,1,256]{2,1,0:T(1,128)} %fold.3), calls=%async_computation.3 | async-start | bytes 65536 | tf_op jit(solution)/shard_map/all_to_all | solution.py:37
  75.0 0.0 collective-permute-done.refs_1_
  75.1 0.0 collective-permute-done.1.refs_2_
  75.1 3.0 %collective-permute-done.2.refs_3_ = bf16[64,2048]{1,0:T(8,128)(2,1)S(1)} collective-permute-done((bf16[64,2048]{1,0:T(8,128)(2,1)}, bf16[64,2048]{1,0:T(8,128)(2,1)S(1)}, u32[]{:S(2)}, u32[]{:S(2)}) %collective-permute-start.2) | collective-permute-done | bytes 262176 | tf_op jit(solution)/shard_map/ppermute | solution.py:344
  78.1 0.0 copy-done.4
  78.1 0.8 %combine.1 = (bf16[1,64,1024]{2,1,0:T(8,128)(2,1)}, bf16[1,64,1024]{2,1,0:T(8,128)(2,1)}) custom-call(bf16[64,2048]{1,0:T(8,128)(2,1)S(1)} %copy-done.4, bf16[64,2048]{1,0:T(8,128)(2,1)S(1)} %collective-permute-done.refs_1_, bf16[64,2048]{1,0:T(8,128)(2,1)S(1)} %collective-permute-done.1.refs_2_, bf16[64,2048]{1,0:T(8,128)(2,1)S(1)} %collective-permute-done.2.refs_3_), custom_call_target="tpu_custom_call" | custom-call | flops 262144 | bytes 1310720 | tf_op jit(solution)/shard_map/combine/pallas_call | solution.py:349
  78.9 0.5 all-to-all-done.3
  79.4 0.6 copy.14
  (1 shorter events, 0.0 us)
Async XLA Ops:
  2.7 5.8 %copy-start.8 = (s32[1,64]{1,0:T(1,128)S(1)}, s32[1,64]{1,0:T(1,128)}, u32[]{:S(2)}) copy-start(s32[1,64]{1,0:T(1,128)} %place_ref.1) | copy-start | bytes 772
  2.7 15.4 %copy-start.1 = (bf16[1,64,8192]{2,1,0:T(8,128)(2,1)S(1)}, bf16[1,64,8192]{2,1,0:T(8,128)(2,1)}, u32[]{:S(2)}) copy-start(bf16[1,64,8192]{2,1,0:T(8,128)(2,1)} %q_ref.3) | copy-start | bytes 3145732
  2.7 15.4 %copy-start.2 = (bf16[1,64,8192]{2,1,0:T(8,128)(2,1)S(1)}, bf16[1,64,8192]{2,1,0:T(8,128)(2,1)}, u32[]{:S(2)}) copy-start(bf16[1,64,8192]{2,1,0:T(8,128)(2,1)} %grad_ref.3) | copy-start | bytes 3145732
  2.8 15.3 %all-to-all-start = ((bf16[4,64,2176]{2,1,0:T(8,128)(2,1)}), bf16[4,64,2176]{2,1,0:T(8,128)(2,1)S(1)}, u32[]{:S(2)}, u32[]{:S(2)}) async-start(bf16[4,64,2176]{2,1,0:T(8,128)(2,1)} %pack.1), calls=%async_computation | async-start | bytes 2228224 | tf_op jit(solution)/shard_map/all_to_all | solution.py:37
  8.7 11.4 %copy-start.7 = (s32[1,512]{1,0:T(1,128)}, s32[1,512]{1,0:T(1,128)S(1)}, u32[]{:S(2)}) copy-start(s32[1,512]{1,0:T(1,128)S(1)} %tile.13.qp_ref) | copy-start | bytes 6148
  8.7 11.4 %copy-start.6 = (f32[8192]{0:T(1024)S(1)}, f32[8192]{0:T(1024)}, u32[]{:S(2)}) copy-start(f32[8192]{0:T(1024)} %param.15) | copy-start | bytes 98308
  18.1 2.0 %copy-start = (bf16[4,64,2176]{2,1,0:T(8,128)(2,1)}, bf16[4,64,2176]{2,1,0:T(8,128)(2,1)S(1)}, u32[]{:S(2)}) copy-start(bf16[4,64,2176]{2,1,0:T(8,128)(2,1)S(1)} %all-to-all-done.pay_ref.k_ref.v_ref.kp_ref) | copy-start | bytes 3342340
  18.1 2.0 %copy-start.3 = (bf16[1,64,8192]{2,1,0:T(8,128)(2,1)S(1)}, bf16[1,64,8192]{2,1,0:T(8,128)(2,1)}, u32[]{:S(2)}) copy-start(bf16[1,64,8192]{2,1,0:T(8,128)(2,1)} %hidden_ref.1) | copy-start | bytes 3145732
  21.3 0.6 copy-start.5
  21.9 20.1 %all-to-all-start.1 = ((f32[32,1,256]{2,1,0:T(1,128)}), f32[32,1,256]{2,1,0:T(1,128)S(1)}, u32[]{:S(2)}, u32[]{:S(2)}) async-start(f32[32,1,256]{2,1,0:T(1,128)} %get-tuple-element.22), calls=%async_computation.1 | async-start | bytes 65536 | tf_op jit(solution)/shard_map/all_to_all | solution.py:37
  42.6 20.5 %all-to-all-start.2 = ((f32[16,1,256]{2,1,0:T(1,128)}), f32[16,1,256]{2,1,0:T(1,128)S(1)}, u32[]{:S(2)}, u32[]{:S(2)}) async-start(f32[16,1,256]{2,1,0:T(1,128)} %fold.2), calls=%async_computation.2 | async-start | bytes 32768 | tf_op jit(solution)/shard_map/all_to_all | solution.py:37
  59.1 18.9 %copy-start.4 = (bf16[64,2048]{1,0:T(8,128)(2,1)S(1)}, bf16[64,2048]{1,0:T(8,128)(2,1)}, u32[]{:S(2)}) copy-start(bf16[64,2048]{1,0:T(8,128)(2,1)} %get-tuple-element.28.refs_0_) | copy-start | bytes 786436
  59.1 15.9 %collective-permute-start = (bf16[64,2048]{1,0:T(8,128)(2,1)}, bf16[64,2048]{1,0:T(8,128)(2,1)S(1)}, u32[]{:S(2)}, u32[]{:S(2)}) collective-permute-start(bf16[64,2048]{1,0:T(8,128)(2,1)} %get-tuple-element.29), channel_id=1, source_target_pairs={{1,0},{2,1},{3,2},{5,4},{6,5},{7,6},{9,8},{10,9},{11,10},{13,12},{... | collective-permute-start | bytes 786440 | tf_op jit(solution)/shard_map/ppermute | solution.py:344
  60.6 14.5 %collective-permute-start.1 = (bf16[64,2048]{1,0:T(8,128)(2,1)}, bf16[64,2048]{1,0:T(8,128)(2,1)S(1)}, u32[]{:S(2)}, u32[]{:S(2)}) collective-permute-start(bf16[64,2048]{1,0:T(8,128)(2,1)} %get-tuple-element.30), channel_id=1, source_target_pairs={{2,0},{3,1},{6,4},{7,5},{10,8},{11,9},{14,12},{15,13},{18,16},{19,... | collective-permute-start | bytes 786440 | tf_op jit(solution)/shard_map/ppermute | solution.py:344
  61.9 16.2 %collective-permute-start.2 = (bf16[64,2048]{1,0:T(8,128)(2,1)}, bf16[64,2048]{1,0:T(8,128)(2,1)S(1)}, u32[]{:S(2)}, u32[]{:S(2)}) collective-permute-start(bf16[64,2048]{1,0:T(8,128)(2,1)} %get-tuple-element.31), channel_id=1, source_target_pairs={{3,0},{7,4},{11,8},{15,12},{19,16},{23,20},{27,24},{31,28},{35,32}... | collective-permute-start | bytes 786440 | tf_op jit(solution)/shard_map/ppermute | solution.py:344
  63.8 15.5 %all-to-all-start.3 = ((f32[32,1,256]{2,1,0:T(1,128)}), f32[32,1,256]{2,1,0:T(1,128)S(1)}, u32[]{:S(2)}, u32[]{:S(2)}) async-start(f32[32,1,256]{2,1,0:T(1,128)} %fold.3), calls=%async_computation.3 | async-start | bytes 65536 | tf_op jit(solution)/shard_map/all_to_all | solution.py:37

commit v5 on v4

--- a/solution.py
+++ b/solution.py
@@ -17,9 +17,10 @@
 LOG2_SCALE = SCALE * math.log2(math.e)
 X, Z, CORES, Y = 4, 16, 2, 4
 PLANE = X * CORES * Y
-Y_FIRST, Z_FIRST, PLANE_FIRST = 0, 10, 17
+Y_FIRST, Z_FIRST, SUM_FIRST, SPREAD_FIRST = 0, 12, 17, 19
 VMEM_LIMIT = 48 * 1024 * 1024
 FULL_VMEM = 60 * 1024 * 1024
+BACKWARD_VMEM = 53 * 1024 * 1024
 FOLD_FLOPS = 1 << 35
 HBM = pl.BlockSpec(memory_space=pltpu.HBM)
 NT = (((1,), (1,)), ((), ()))
@@ -141,8 +142,9 @@
     logit_grad = along_ref[...] * slope * (1.0 / math.sqrt(X * Z * CORES * Y * rows))
     chunk = out_ref.shape[2]
     for part in range(PLANE):
+        column = (part + SUM_FIRST - SPREAD_FIRST) % PLANE * chunk
         for lane in range(0, chunk, 128):
-            left = part * chunk + lane
+            left = column + lane
             block = hidden_ref[0, :, left : left + 128].astype(jnp.float32)
             out_ref[part, :, lane : lane + 128] = jnp.sum(
                 block * logit_grad, axis=0, keepdims=True
@@ -318,7 +320,7 @@
             whole(rows, 128),
         ],
         out_specs=[wide_block] + [pl.BlockSpec((rows, 2 * span), lambda i: (0, i))] * Y,
-        compiler_params=params(FULL_VMEM),
+        compiler_params=params(BACKWARD_VMEM),
         cost_estimate=pl.CostEstimate(
             flops=10 * rows * width * Y * rows,
             bytes_accessed=6 * rows * width,
@@ -336,7 +338,7 @@
     )
 
     plane = ("x", "core", "ctx")
-    shares = exchange(term, plane, PLANE_FIRST)
+    shares = exchange(term, plane, SUM_FIRST)
     share = fold(shares, Z, 8192)
     share, *terms = lax.optimization_barrier((share, *terms))
     lines = exchange(share, "z", Z_FIRST)
@@ -345,7 +347,7 @@
         for back in range(1, Y)
     ]
     line = fold(lines, PLANE, FOLD_FLOPS)
-    router_grad = exchange(line, plane, PLANE_FIRST).reshape(width)
+    router_grad = exchange(line, plane, SPREAD_FIRST).reshape(width)
     key_gradient, value_gradient = pl.pallas_call(
         functools.partial(combine_kernel, span),
         out_shape=[jax.ShapeDtypeStruct((1, rows, KV_WIDTH), jnp.bfloat16)] * 2,

time: 80.4 us -> 77.8 us (0.968)
  starting transfers between devices: 49.7 us -> 45.3 us
  waiting for transfers between devices: 12.9 us -> 15.3 us
    all_to_all x4, starting transfers between devices: 45.7 us -> 41.4 us  [exchange(): lax.all_to_all(parts, axis, 0, 0, axis_index_groups=[order], tiled=True)]
    all_to_all x4, waiting for transfers between devices: 9.92 us -> 12.3 us  [exchange(): lax.all_to_all(parts, axis, 0, 0, axis_index_groups=[order], tiled=True)]
where the time goes in v5:
time: 77.8 us; the launch traced here: 77.4 us
  starting transfers between devices  45.3 us (58%)
  waiting for transfers between devices  15.3 us (20%)
  Pallas kernels  14.6 us (19%)
  between operations  1.41 us (2%)
    all_to_all x4, starting transfers between devices, exchange(): lax.all_to_all(parts, axis, 0, 0, axis_index_groups=[order], tiled=True)  41.4 us
    all_to_all x4, waiting for transfers between devices, exchange(): lax.all_to_all(parts, axis, 0, 0, axis_index_groups=[order], tiled=True)  12.3 us
    pallas_call x1, Pallas kernels, body(): pl.pallas_call(functools.partial(backward_kernel, heads), grid=(steps,),...  7.32 us
    ppermute x3, starting transfers between devices, body(): lax.ppermute(terms[back], 'ctx', [(i, i - back) for i in range(back, Y)])  3.86 us
    ppermute x3, waiting for transfers between devices, body(): lax.ppermute(terms[back], 'ctx', [(i, i - back) for i in range(back, Y)])  3.05 us
    pallas_call x1, Pallas kernels, body(): pl.pallas_call(pack_kernel, out_shape=jax.ShapeDtypeStruct((Y, rows, 2 *...  2.06 us
    pallas_call x1, Pallas kernels, body(): pl.pallas_call(forward_kernel, out_shape=jax.ShapeDtypeStruct((rows, 128)...  1.96 us
  transfers between devices with their start and end apart: 7, of which 3 were waited for; matrix products, arithmetic and copies ran while one was open for 0% of the time, Pallas kernels for 11%

profile of v5, /device:TPU:1, one launch (start us, length us, event | category | flops | bytes accessed | tf_op | source)
XLA Modules:
  0.0 77.4 jit_solution(1313074233160821924)
XLA Ops:
  0.6 2.1 %pack.1 = bf16[4,64,2176]{2,1,0:T(8,128)(2,1)} custom-call(bf16[1,64,1024]{2,1,0:T(8,128)(2,1)} %key_ref.1, bf16[1,64,1024]{2,1,0:T(8,128)(2,1)} %value_ref.1, s32[1,64]{1,0:T(1,128)} %place_ref.1), custom_call_target="tpu_custom_call" | custom-call | tf_op jit(solution)/shard_map/pack/pallas_call | solution.py:251
  2.7 0.0 copy-start.5
  2.7 0.0 copy-start.1
  2.7 0.0 copy-start.2
  2.7 5.2 %all-to-all-start = ((bf16[4,64,2176]{2,1,0:T(8,128)(2,1)}), bf16[4,64,2176]{2,1,0:T(8,128)(2,1)S(1)}, u32[]{:S(2)}, u32[]{:S(2)}) async-start(bf16[4,64,2176]{2,1,0:T(8,128)(2,1)} %pack.1), calls=%async_computation | async-start | bytes 2228224 | tf_op jit(solution)/shard_map/all_to_all | solution.py:38
  8.5 0.0 copy-done.5
  8.6 0.1 tile.13.qp_ref
  8.6 0.0 copy-start.4
  8.6 9.4 %all-to-all-done.pay_ref.k_ref.v_ref.kp_ref = bf16[4,64,2176]{2,1,0:T(8,128)(2,1)S(1)} async-done(((bf16[4,64,2176]{2,1,0:T(8,128)(2,1)}), bf16[4,64,2176]{2,1,0:T(8,128)(2,1)S(1)}, u32[]{:S(2)}, u32[]{:S(2)}) %all-to-all-start) | async-done | bytes 1114144 | tf_op jit(solution)/shard_map/all_to_all | solution.py:38
  18.1 0.0 copy-done.1
  18.1 0.0 copy-done.2
  18.1 0.0 copy-start
  18.1 0.0 copy-start.3
  18.1 2.0 %forward.1.along_ref = f32[64,128]{1,0:T(8,128)S(1)} custom-call(bf16[1,64,8192]{2,1,0:T(8,128)(2,1)S(1)} %copy-done.1, bf16[1,64,8192]{2,1,0:T(8,128)(2,1)S(1)} %copy-done.2, bf16[4,64,2176]{2,1,0:T(8,128)(2,1)S(1)} %all-to-all-done.pay_ref.k_ref.v_ref.kp_ref, s32[1,512]{1,0:T(1,128)S(1)} %tile.13.qp_ref), custom_call_target="tpu_custom_call" | custom-call | flops 536870912 | bytes 3145728 | tf_op jit(solution)/shard_map/forward/pallas_call | solution.py:279
  20.0 0.0 copy-done
  20.0 0.0 copy-done.4
  20.0 0.0 copy-done.3
  20.1 1.2 %router.1 = (f32[32,1,256]{2,1,0:T(1,128)}, f32[64,128]{1,0:T(8,128)S(1)}) custom-call(f32[64,128]{1,0:T(8,128)S(1)} %forward.1.along_ref, bf16[1,64,8192]{2,1,0:T(8,128)(2,1)S(1)} %copy-done.3, f32[1,8192]{1,0:T(1,128)S(1)} %bitcast.3, s32[1,1]{1,0:T(1,128)S(6)} %copy.13.count_ref), custom_call_target="tpu_custom_call" | custom-call | flops 2097152 | bytes 1048576 | tf_op jit(solution)/shard_map/router/pallas_call | solution.py:292
  21.2 12.8 %all-to-all-start.1 = ((f32[32,1,256]{2,1,0:T(1,128)}), f32[32,1,256]{2,1,0:T(1,128)S(1)}, u32[]{:S(2)}, u32[]{:S(2)}) async-start(f32[32,1,256]{2,1,0:T(1,128)} %get-tuple-element.22), calls=%async_computation.1 | async-start | bytes 65536 | tf_op jit(solution)/shard_map/all_to_all | solution.py:38
  34.1 7.3 %backward.1 = (bf16[1,64,8192]{2,1,0:T(8,128)(2,1)}, bf16[64,2048]{1,0:T(8,128)(2,1)S(1)}, bf16[64,2048]{1,0:T(8,128)(2,1)S(1)}, bf16[64,2048]{1,0:T(8,128)(2,1)S(1)}, bf16[64,2048]{1,0:T(8,128)(2,1)}) custom-call(bf16[1,64,8192]{2,1,0:T(8,128)(2,1)} %q_ref.3, bf16[1,64,8192]{2,1,0:T(8,128)(2,1)} %grad_ref.3, bf16[4,64,2176]{2,1,0:T(8,128)(2,1)} %copy-done, ...), custom_call_target="tpu_custom_call" | custom-call | flops 1342177280 | bytes 3145728 | tf_op jit(solution)/shard_map/backward/pallas_call | solution.py:306
  41.4 0.0 all-to-all-done.1.share_ref
  41.4 0.6 fold.2
  42.1 15.1 %all-to-all-start.2 = ((f32[16,1,256]{2,1,0:T(1,128)}), f32[16,1,256]{2,1,0:T(1,128)S(1)}, u32[]{:S(2)}, u32[]{:S(2)}) async-start(f32[16,1,256]{2,1,0:T(1,128)} %fold.2), calls=%async_computation.2 | async-start | bytes 32768 | tf_op jit(solution)/shard_map/all_to_all | solution.py:38
  57.2 1.3 %collective-permute-start = (bf16[64,2048]{1,0:T(8,128)(2,1)S(1)}, bf16[64,2048]{1,0:T(8,128)(2,1)S(1)}, u32[]{:S(2)}, u32[]{:S(2)}) collective-permute-start(bf16[64,2048]{1,0:T(8,128)(2,1)S(1)} %get-tuple-element.29), channel_id=1, source_target_pairs={{1,0},{2,1},{3,2},{5,4},{6,5},{7,6},{9,8},{10,9},{11,10},{13,12},{... | collective-permute-start | bytes 786440 | tf_op jit(solution)/shard_map/ppermute | solution.py:346
  58.5 1.3 %collective-permute-start.1 = (bf16[64,2048]{1,0:T(8,128)(2,1)S(1)}, bf16[64,2048]{1,0:T(8,128)(2,1)S(1)}, u32[]{:S(2)}, u32[]{:S(2)}) collective-permute-start(bf16[64,2048]{1,0:T(8,128)(2,1)S(1)} %get-tuple-element.30), channel_id=1, source_target_pairs={{2,0},{3,1},{6,4},{7,5},{10,8},{11,9},{14,12},{15,13},{18,16},{19,... | collective-permute-start | bytes 786440 | tf_op jit(solution)/shard_map/ppermute | solution.py:346
  59.8 1.3 %collective-permute-start.2 = (bf16[64,2048]{1,0:T(8,128)(2,1)}, bf16[64,2048]{1,0:T(8,128)(2,1)S(1)}, u32[]{:S(2)}, u32[]{:S(2)}) collective-permute-start(bf16[64,2048]{1,0:T(8,128)(2,1)} %get-tuple-element.31), channel_id=1, source_target_pairs={{3,0},{7,4},{11,8},{15,12},{19,16},{23,20},{27,24},{31,28},{35,32}... | collective-permute-start | bytes 786440 | tf_op jit(solution)/shard_map/ppermute | solution.py:346
  61.1 2.8 %all-to-all-done.2.share_ref = f32[16,1,256]{2,1,0:T(1,128)S(1)} async-done(((f32[16,1,256]{2,1,0:T(1,128)}), f32[16,1,256]{2,1,0:T(1,128)S(1)}, u32[]{:S(2)}, u32[]{:S(2)}) %all-to-all-start.2) | async-done | bytes 16416 | tf_op jit(solution)/shard_map/all_to_all | solution.py:38
  63.9 0.6 fold.3
  64.5 8.3 %all-to-all-start.3 = ((f32[32,1,256]{2,1,0:T(1,128)}), f32[32,1,256]{2,1,0:T(1,128)S(1)}, u32[]{:S(2)}, u32[]{:S(2)}) async-start(f32[32,1,256]{2,1,0:T(1,128)} %fold.3), calls=%async_computation.3 | async-start | bytes 65536 | tf_op jit(solution)/shard_map/all_to_all | solution.py:38
  72.9 0.0 collective-permute-done.refs_1_
  72.9 0.0 collective-permute-done.1.refs_2_
  72.9 3.0 %collective-permute-done.2.refs_3_ = bf16[64,2048]{1,0:T(8,128)(2,1)S(1)} collective-permute-done((bf16[64,2048]{1,0:T(8,128)(2,1)}, bf16[64,2048]{1,0:T(8,128)(2,1)S(1)}, u32[]{:S(2)}, u32[]{:S(2)}) %collective-permute-start.2) | collective-permute-done | bytes 262176 | tf_op jit(solution)/shard_map/ppermute | solution.py:346
  75.9 0.8 %combine.1 = (bf16[1,64,1024]{2,1,0:T(8,128)(2,1)}, bf16[1,64,1024]{2,1,0:T(8,128)(2,1)}) custom-call(bf16[64,2048]{1,0:T(8,128)(2,1)S(1)} %get-tuple-element.28.refs_0_, bf16[64,2048]{1,0:T(8,128)(2,1)S(1)} %collective-permute-done.refs_1_, bf16[64,2048]{1,0:T(8,128)(2,1)S(1)} %collective-permute-done.1.refs_2_, ...), custom_call_target="tpu_custom_call" | custom-call | flops 262144 | bytes 1310720 | tf_op jit(solution)/shard_map/combine/pallas_call | solution.py:351
  76.8 0.0 all-to-all-done.3
  76.8 0.6 copy.14
  (1 shorter events, 0.0 us)
Async XLA Ops:
  2.7 5.8 %copy-start.5 = (s32[1,64]{1,0:T(1,128)S(1)}, s32[1,64]{1,0:T(1,128)}, u32[]{:S(2)}) copy-start(s32[1,64]{1,0:T(1,128)} %place_ref.1) | copy-start | bytes 772
  2.7 15.4 %copy-start.1 = (bf16[1,64,8192]{2,1,0:T(8,128)(2,1)S(1)}, bf16[1,64,8192]{2,1,0:T(8,128)(2,1)}, u32[]{:S(2)}) copy-start(bf16[1,64,8192]{2,1,0:T(8,128)(2,1)} %q_ref.3) | copy-start | bytes 3145732
  2.7 15.4 %copy-start.2 = (bf16[1,64,8192]{2,1,0:T(8,128)(2,1)S(1)}, bf16[1,64,8192]{2,1,0:T(8,128)(2,1)}, u32[]{:S(2)}) copy-start(bf16[1,64,8192]{2,1,0:T(8,128)(2,1)} %grad_ref.3) | copy-start | bytes 3145732
  2.7 15.3 %all-to-all-start = ((bf16[4,64,2176]{2,1,0:T(8,128)(2,1)}), bf16[4,64,2176]{2,1,0:T(8,128)(2,1)S(1)}, u32[]{:S(2)}, u32[]{:S(2)}) async-start(bf16[4,64,2176]{2,1,0:T(8,128)(2,1)} %pack.1), calls=%async_computation | async-start | bytes 2228224 | tf_op jit(solution)/shard_map/all_to_all | solution.py:38
  8.6 11.4 %copy-start.4 = (f32[8192]{0:T(1024)S(1)}, f32[8192]{0:T(1024)}, u32[]{:S(2)}) copy-start(f32[8192]{0:T(1024)} %param.15) | copy-start | bytes 98308
  18.1 2.0 %copy-start = (bf16[4,64,2176]{2,1,0:T(8,128)(2,1)}, bf16[4,64,2176]{2,1,0:T(8,128)(2,1)S(1)}, u32[]{:S(2)}) copy-start(bf16[4,64,2176]{2,1,0:T(8,128)(2,1)S(1)} %all-to-all-done.pay_ref.k_ref.v_ref.kp_ref) | copy-start | bytes 3342340
  18.1 2.0 %copy-start.3 = (bf16[1,64,8192]{2,1,0:T(8,128)(2,1)S(1)}, bf16[1,64,8192]{2,1,0:T(8,128)(2,1)}, u32[]{:S(2)}) copy-start(bf16[1,64,8192]{2,1,0:T(8,128)(2,1)} %hidden_ref.1) | copy-start | bytes 3145732
  21.2 20.2 %all-to-all-start.1 = ((f32[32,1,256]{2,1,0:T(1,128)}), f32[32,1,256]{2,1,0:T(1,128)S(1)}, u32[]{:S(2)}, u32[]{:S(2)}) async-start(f32[32,1,256]{2,1,0:T(1,128)} %get-tuple-element.22), calls=%async_computation.1 | async-start | bytes 65536 | tf_op jit(solution)/shard_map/all_to_all | solution.py:38
  42.1 21.8 %all-to-all-start.2 = ((f32[16,1,256]{2,1,0:T(1,128)}), f32[16,1,256]{2,1,0:T(1,128)S(1)}, u32[]{:S(2)}, u32[]{:S(2)}) async-start(f32[16,1,256]{2,1,0:T(1,128)} %fold.2), calls=%async_computation.2 | async-start | bytes 32768 | tf_op jit(solution)/shard_map/all_to_all | solution.py:38
  57.2 15.7 %collective-permute-start = (bf16[64,2048]{1,0:T(8,128)(2,1)S(1)}, bf16[64,2048]{1,0:T(8,128)(2,1)S(1)}, u32[]{:S(2)}, u32[]{:S(2)}) collective-permute-start(bf16[64,2048]{1,0:T(8,128)(2,1)S(1)} %get-tuple-element.29), channel_id=1, source_target_pairs={{1,0},{2,1},{3,2},{5,4},{6,5},{7,6},{9,8},{10,9},{11,10},{13,12},{... | collective-permute-start | bytes 786440 | tf_op jit(solution)/shard_map/ppermute | solution.py:346
  58.5 14.4 %collective-permute-start.1 = (bf16[64,2048]{1,0:T(8,128)(2,1)S(1)}, bf16[64,2048]{1,0:T(8,128)(2,1)S(1)}, u32[]{:S(2)}, u32[]{:S(2)}) collective-permute-start(bf16[64,2048]{1,0:T(8,128)(2,1)S(1)} %get-tuple-element.30), channel_id=1, source_target_pairs={{2,0},{3,1},{6,4},{7,5},{10,8},{11,9},{14,12},{15,13},{18,16},{19,... | collective-permute-start | bytes 786440 | tf_op jit(solution)/shard_map/ppermute | solution.py:346
  59.8 16.2 %collective-permute-start.2 = (bf16[64,2048]{1,0:T(8,128)(2,1)}, bf16[64,2048]{1,0:T(8,128)(2,1)S(1)}, u32[]{:S(2)}, u32[]{:S(2)}) collective-permute-start(bf16[64,2048]{1,0:T(8,128)(2,1)} %get-tuple-element.31), channel_id=1, source_target_pairs={{3,0},{7,4},{11,8},{15,12},{19,16},{23,20},{27,24},{31,28},{35,32}... | collective-permute-start | bytes 786440 | tf_op jit(solution)/shard_map/ppermute | solution.py:346
  64.5 12.2 %all-to-all-start.3 = ((f32[32,1,256]{2,1,0:T(1,128)}), f32[32,1,256]{2,1,0:T(1,128)S(1)}, u32[]{:S(2)}, u32[]{:S(2)}) async-start(f32[32,1,256]{2,1,0:T(1,128)} %fold.3), calls=%async_computation.3 | async-start | bytes 65536 | tf_op jit(solution)/shard_map/all_to_all | solution.py:38

commit v6 on v5

--- a/solution.py
+++ b/solution.py
@@ -17,7 +17,7 @@
 LOG2_SCALE = SCALE * math.log2(math.e)
 X, Z, CORES, Y = 4, 16, 2, 4
 PLANE = X * CORES * Y
-Y_FIRST, Z_FIRST, SUM_FIRST, SPREAD_FIRST = 0, 12, 17, 19
+Y_FIRST, Z_FIRST, SUM_FIRST, SPREAD_FIRST = 0, 11, 17, 19
 VMEM_LIMIT = 48 * 1024 * 1024
 FULL_VMEM = 60 * 1024 * 1024
 BACKWARD_VMEM = 53 * 1024 * 1024
@@ -265,7 +265,7 @@
     gathered = exchange(payload, "ctx", Y_FIRST)
 
     query_places = jnp.tile(positions, (1, GROUP))
-    heads = 2
+    heads = 4
     steps = KEY_VALUE_HEADS // heads
     span = heads * HEAD_SIZE
     wide_block = pl.BlockSpec((1, rows, heads * GROUP * HEAD_SIZE), lambda i: (0, 0, i))
@@ -344,7 +344,7 @@
     lines = exchange(share, "z", Z_FIRST)
     term_shares = [terms[0]] + [
         lax.ppermute(terms[back], "ctx", [(i, i - back) for i in range(back, Y)])
-        for back in range(1, Y)
+        for back in (2, 3, 1)
     ]
     line = fold(lines, PLANE, FOLD_FLOPS)
     router_grad = exchange(line, plane, SPREAD_FIRST).reshape(width)

time: 77.8 us -> 76.9 us (0.988)
  waiting for transfers between devices: 15.3 us -> 13.4 us
  starting transfers between devices: 45.3 us -> 46.5 us
    all_to_all x4, waiting for transfers between devices: 12.3 us -> 10.1 us  [exchange(): lax.all_to_all(parts, axis, 0, 0, axis_index_groups=[order], tiled=True)]
    all_to_all x4, starting transfers between devices: 41.4 us -> 42.6 us  [exchange(): lax.all_to_all(parts, axis, 0, 0, axis_index_groups=[order], tiled=True)]
where the time goes in v6:
time: 76.9 us; the launch traced here: 76.5 us
  starting transfers between devices  46.5 us (60%)
  Pallas kernels  14.5 us (19%)
  waiting for transfers between devices  13.4 us (17%)
  between operations  1.41 us (2%)
    all_to_all x4, starting transfers between devices, exchange(): lax.all_to_all(parts, axis, 0, 0, axis_index_groups=[order], tiled=True)  42.6 us
    all_to_all x4, waiting for transfers between devices, exchange(): lax.all_to_all(parts, axis, 0, 0, axis_index_groups=[order], tiled=True)  10.1 us
    pallas_call x1, Pallas kernels, body(): pl.pallas_call(functools.partial(backward_kernel, heads), grid=(steps,),...  7.19 us
    ppermute x3, starting transfers between devices, body(): lax.ppermute(terms[back], 'ctx', [(i, i - back) for i in range(back, Y)])  3.86 us
    ppermute x3, waiting for transfers between devices, body(): lax.ppermute(terms[back], 'ctx', [(i, i - back) for i in range(back, Y)])  3.27 us
    pallas_call x1, Pallas kernels, body(): pl.pallas_call(pack_kernel, out_shape=jax.ShapeDtypeStruct((Y, rows, 2 *...  2.06 us
    pallas_call x1, Pallas kernels, body(): pl.pallas_call(forward_kernel, out_shape=jax.ShapeDtypeStruct((rows, 128)...  1.96 us
  transfers between devices with their start and end apart: 7, of which 3 were waited for; matrix products, arithmetic and copies ran while one was open for 0% of the time, Pallas kernels for 11%

profile of v6, /device:TPU:1, one launch (start us, length us, event | category | flops | bytes accessed | tf_op | source)
XLA Modules:
  0.0 76.5 jit_solution(17408192192117105313)
XLA Ops:
  0.6 2.1 %pack.1 = bf16[4,64,2176]{2,1,0:T(8,128)(2,1)} custom-call(bf16[1,64,1024]{2,1,0:T(8,128)(2,1)} %key_ref.1, bf16[1,64,1024]{2,1,0:T(8,128)(2,1)} %value_ref.1, s32[1,64]{1,0:T(1,128)} %place_ref.1), custom_call_target="tpu_custom_call" | custom-call | tf_op jit(solution)/shard_map/pack/pallas_call | solution.py:251
  2.7 0.0 copy-start.5
  2.7 0.0 copy-start.1
  2.7 0.0 copy-start.2
  2.7 5.2 %all-to-all-start = ((bf16[4,64,2176]{2,1,0:T(8,128)(2,1)}), bf16[4,64,2176]{2,1,0:T(8,128)(2,1)S(1)}, u32[]{:S(2)}, u32[]{:S(2)}) async-start(bf16[4,64,2176]{2,1,0:T(8,128)(2,1)} %pack.1), calls=%async_computation | async-start | bytes 2228224 | tf_op jit(solution)/shard_map/all_to_all | solution.py:38
  8.5 0.0 copy-done.5
  8.6 0.1 tile.13.qp_ref
  8.6 0.0 copy-start.4
  8.6 9.4 %all-to-all-done.pay_ref.k_ref.v_ref.kp_ref = bf16[4,64,2176]{2,1,0:T(8,128)(2,1)S(1)} async-done(((bf16[4,64,2176]{2,1,0:T(8,128)(2,1)}), bf16[4,64,2176]{2,1,0:T(8,128)(2,1)S(1)}, u32[]{:S(2)}, u32[]{:S(2)}) %all-to-all-start) | async-done | bytes 1114144 | tf_op jit(solution)/shard_map/all_to_all | solution.py:38
  18.1 0.0 copy-done.1
  18.1 0.0 copy-done.2
  18.1 0.0 copy-start
  18.1 0.0 copy-start.3
  18.1 2.0 %forward.1.along_ref = f32[64,128]{1,0:T(8,128)S(1)} custom-call(bf16[1,64,8192]{2,1,0:T(8,128)(2,1)S(1)} %copy-done.1, bf16[1,64,8192]{2,1,0:T(8,128)(2,1)S(1)} %copy-done.2, bf16[4,64,2176]{2,1,0:T(8,128)(2,1)S(1)} %all-to-all-done.pay_ref.k_ref.v_ref.kp_ref, s32[1,512]{1,0:T(1,128)S(1)} %tile.13.qp_ref), custom_call_target="tpu_custom_call" | custom-call | flops 536870912 | bytes 3145728 | tf_op jit(solution)/shard_map/forward/pallas_call | solution.py:279
  20.0 0.0 copy-done
  20.0 0.0 copy-done.4
  20.0 0.0 copy-done.3
  20.1 1.2 %router.1 = (f32[32,1,256]{2,1,0:T(1,128)}, f32[64,128]{1,0:T(8,128)S(1)}) custom-call(f32[64,128]{1,0:T(8,128)S(1)} %forward.1.along_ref, bf16[1,64,8192]{2,1,0:T(8,128)(2,1)S(1)} %copy-done.3, f32[1,8192]{1,0:T(1,128)S(1)} %bitcast.3, s32[1,1]{1,0:T(1,128)S(6)} %copy.13.count_ref), custom_call_target="tpu_custom_call" | custom-call | flops 2097152 | bytes 1048576 | tf_op jit(solution)/shard_map/router/pallas_call | solution.py:292
  21.2 12.8 %all-to-all-start.1 = ((f32[32,1,256]{2,1,0:T(1,128)}), f32[32,1,256]{2,1,0:T(1,128)S(1)}, u32[]{:S(2)}, u32[]{:S(2)}) async-start(f32[32,1,256]{2,1,0:T(1,128)} %get-tuple-element.22), calls=%async_computation.1 | async-start | bytes 65536 | tf_op jit(solution)/shard_map/all_to_all | solution.py:38
  34.1 7.2 %backward.1 = (bf16[1,64,8192]{2,1,0:T(8,128)(2,1)}, bf16[64,2048]{1,0:T(8,128)(2,1)S(1)}, bf16[64,2048]{1,0:T(8,128)(2,1)S(1)}, bf16[64,2048]{1,0:T(8,128)(2,1)S(1)}, bf16[64,2048]{1,0:T(8,128)(2,1)}) custom-call(bf16[1,64,8192]{2,1,0:T(8,128)(2,1)} %q_ref.3, bf16[1,64,8192]{2,1,0:T(8,128)(2,1)} %grad_ref.3, bf16[4,64,2176]{2,1,0:T(8,128)(2,1)} %copy-done, ...), custom_call_target="tpu_custom_call" | custom-call | flops 1342177280 | bytes 3145728 | tf_op jit(solution)/shard_map/backward/pallas_call | solution.py:306
  41.3 0.0 all-to-all-done.1.share_ref
  41.3 0.6 fold.2
  41.9 15.6 %all-to-all-start.2 = ((f32[16,1,256]{2,1,0:T(1,128)}), f32[16,1,256]{2,1,0:T(1,128)S(1)}, u32[]{:S(2)}, u32[]{:S(2)}) async-start(f32[16,1,256]{2,1,0:T(1,128)} %fold.2), calls=%async_computation.2 | async-start | bytes 32768 | tf_op jit(solution)/shard_map/all_to_all | solution.py:38
  57.5 1.3 %collective-permute-start = (bf16[64,2048]{1,0:T(8,128)(2,1)S(1)}, bf16[64,2048]{1,0:T(8,128)(2,1)S(1)}, u32[]{:S(2)}, u32[]{:S(2)}) collective-permute-start(bf16[64,2048]{1,0:T(8,128)(2,1)S(1)} %get-tuple-element.29), channel_id=1, source_target_pairs={{2,0},{3,1},{6,4},{7,5},{10,8},{11,9},{14,12},{15,13},{18,16},{19,... | collective-permute-start | bytes 786440 | tf_op jit(solution)/shard_map/ppermute | solution.py:346
  58.8 1.3 %collective-permute-start.1 = (bf16[64,2048]{1,0:T(8,128)(2,1)}, bf16[64,2048]{1,0:T(8,128)(2,1)S(1)}, u32[]{:S(2)}, u32[]{:S(2)}) collective-permute-start(bf16[64,2048]{1,0:T(8,128)(2,1)} %get-tuple-element.30), channel_id=1, source_target_pairs={{3,0},{7,4},{11,8},{15,12},{19,16},{23,20},{27,24},{31,28},{35,32}... | collective-permute-start | bytes 786440 | tf_op jit(solution)/shard_map/ppermute | solution.py:346
  60.1 1.3 %collective-permute-start.2 = (bf16[64,2048]{1,0:T(8,128)(2,1)S(1)}, bf16[64,2048]{1,0:T(8,128)(2,1)S(1)}, u32[]{:S(2)}, u32[]{:S(2)}) collective-permute-start(bf16[64,2048]{1,0:T(8,128)(2,1)S(1)} %get-tuple-element.31), channel_id=1, source_target_pairs={{1,0},{2,1},{3,2},{5,4},{6,5},{7,6},{9,8},{10,9},{11,10},{13,12},{... | collective-permute-start | bytes 786440 | tf_op jit(solution)/shard_map/ppermute | solution.py:346
  61.4 0.7 all-to-all-done.2.share_ref
  62.1 0.6 fold.3
  62.7 9.0 %all-to-all-start.3 = ((f32[32,1,256]{2,1,0:T(1,128)}), f32[32,1,256]{2,1,0:T(1,128)S(1)}, u32[]{:S(2)}, u32[]{:S(2)}) async-start(f32[32,1,256]{2,1,0:T(1,128)} %fold.3), calls=%async_computation.3 | async-start | bytes 65536 | tf_op jit(solution)/shard_map/all_to_all | solution.py:38
  71.8 0.0 collective-permute-done.refs_1_
  71.8 3.3 %collective-permute-done.1.refs_2_ = bf16[64,2048]{1,0:T(8,128)(2,1)S(1)} collective-permute-done((bf16[64,2048]{1,0:T(8,128)(2,1)}, bf16[64,2048]{1,0:T(8,128)(2,1)S(1)}, u32[]{:S(2)}, u32[]{:S(2)}) %collective-permute-start.1) | collective-permute-done | bytes 262176 | tf_op jit(solution)/shard_map/ppermute | solution.py:346
  75.0 0.0 collective-permute-done.2.refs_3_
  75.1 0.8 %combine.1 = (bf16[1,64,1024]{2,1,0:T(8,128)(2,1)}, bf16[1,64,1024]{2,1,0:T(8,128)(2,1)}) custom-call(bf16[64,2048]{1,0:T(8,128)(2,1)S(1)} %get-tuple-element.28.refs_0_, bf16[64,2048]{1,0:T(8,128)(2,1)S(1)} %collective-permute-done.refs_1_, bf16[64,2048]{1,0:T(8,128)(2,1)S(1)} %collective-permute-done.1.refs_2_, ...), custom_call_target="tpu_custom_call" | custom-call | flops 262144 | bytes 1310720 | tf_op jit(solution)/shard_map/combine/pallas_call | solution.py:351
  75.8 0.0 all-to-all-done.3
  75.9 0.6 copy.14
  (1 shorter events, 0.0 us)
Async XLA Ops:
  2.7 5.8 %copy-start.5 = (s32[1,64]{1,0:T(1,128)S(1)}, s32[1,64]{1,0:T(1,128)}, u32[]{:S(2)}) copy-start(s32[1,64]{1,0:T(1,128)} %place_ref.1) | copy-start | bytes 772
  2.7 15.4 %copy-start.1 = (bf16[1,64,8192]{2,1,0:T(8,128)(2,1)S(1)}, bf16[1,64,8192]{2,1,0:T(8,128)(2,1)}, u32[]{:S(2)}) copy-start(bf16[1,64,8192]{2,1,0:T(8,128)(2,1)} %q_ref.3) | copy-start | bytes 3145732
  2.7 15.4 %copy-start.2 = (bf16[1,64,8192]{2,1,0:T(8,128)(2,1)S(1)}, bf16[1,64,8192]{2,1,0:T(8,128)(2,1)}, u32[]{:S(2)}) copy-start(bf16[1,64,8192]{2,1,0:T(8,128)(2,1)} %grad_ref.3) | copy-start | bytes 3145732
  2.7 15.3 %all-to-all-start = ((bf16[4,64,2176]{2,1,0:T(8,128)(2,1)}), bf16[4,64,2176]{2,1,0:T(8,128)(2,1)S(1)}, u32[]{:S(2)}, u32[]{:S(2)}) async-start(bf16[4,64,2176]{2,1,0:T(8,128)(2,1)} %pack.1), calls=%async_computation | async-start | bytes 2228224 | tf_op jit(solution)/shard_map/all_to_all | solution.py:38
  8.6 11.4 %copy-start.4 = (f32[8192]{0:T(1024)S(1)}, f32[8192]{0:T(1024)}, u32[]{:S(2)}) copy-start(f32[8192]{0:T(1024)} %param.15) | copy-start | bytes 98308
  18.1 2.0 %copy-start = (bf16[4,64,2176]{2,1,0:T(8,128)(2,1)}, bf16[4,64,2176]{2,1,0:T(8,128)(2,1)S(1)}, u32[]{:S(2)}) copy-start(bf16[4,64,2176]{2,1,0:T(8,128)(2,1)S(1)} %all-to-all-done.pay_ref.k_ref.v_ref.kp_ref) | copy-start | bytes 3342340
  18.1 2.0 %copy-start.3 = (bf16[1,64,8192]{2,1,0:T(8,128)(2,1)S(1)}, bf16[1,64,8192]{2,1,0:T(8,128)(2,1)}, u32[]{:S(2)}) copy-start(bf16[1,64,8192]{2,1,0:T(8,128)(2,1)} %hidden_ref.1) | copy-start | bytes 3145732
  21.2 20.0 %all-to-all-start.1 = ((f32[32,1,256]{2,1,0:T(1,128)}), f32[32,1,256]{2,1,0:T(1,128)S(1)}, u32[]{:S(2)}, u32[]{:S(2)}) async-start(f32[32,1,256]{2,1,0:T(1,128)} %get-tuple-element.22), calls=%async_computation.1 | async-start | bytes 65536 | tf_op jit(solution)/shard_map/all_to_all | solution.py:38
  41.9 20.2 %all-to-all-start.2 = ((f32[16,1,256]{2,1,0:T(1,128)}), f32[16,1,256]{2,1,0:T(1,128)S(1)}, u32[]{:S(2)}, u32[]{:S(2)}) async-start(f32[16,1,256]{2,1,0:T(1,128)} %fold.2), calls=%async_computation.2 | async-start | bytes 32768 | tf_op jit(solution)/shard_map/all_to_all | solution.py:38
  57.5 14.3 %collective-permute-start = (bf16[64,2048]{1,0:T(8,128)(2,1)S(1)}, bf16[64,2048]{1,0:T(8,128)(2,1)S(1)}, u32[]{:S(2)}, u32[]{:S(2)}) collective-permute-start(bf16[64,2048]{1,0:T(8,128)(2,1)S(1)} %get-tuple-element.29), channel_id=1, source_target_pairs={{2,0},{3,1},{6,4},{7,5},{10,8},{11,9},{14,12},{15,13},{18,16},{19,... | collective-permute-start | bytes 786440 | tf_op jit(solution)/shard_map/ppermute | solution.py:346
  58.8 16.2 %collective-permute-start.1 = (bf16[64,2048]{1,0:T(8,128)(2,1)}, bf16[64,2048]{1,0:T(8,128)(2,1)S(1)}, u32[]{:S(2)}, u32[]{:S(2)}) collective-permute-start(bf16[64,2048]{1,0:T(8,128)(2,1)} %get-tuple-element.30), channel_id=1, source_target_pairs={{3,0},{7,4},{11,8},{15,12},{19,16},{23,20},{27,24},{31,28},{35,32}... | collective-permute-start | bytes 786440 | tf_op jit(solution)/shard_map/ppermute | solution.py:346
  60.1 14.9 %collective-permute-start.2 = (bf16[64,2048]{1,0:T(8,128)(2,1)S(1)}, bf16[64,2048]{1,0:T(8,128)(2,1)S(1)}, u32[]{:S(2)}, u32[]{:S(2)}) collective-permute-start(bf16[64,2048]{1,0:T(8,128)(2,1)S(1)} %get-tuple-element.31), channel_id=1, source_target_pairs={{1,0},{2,1},{3,2},{5,4},{6,5},{7,6},{9,8},{10,9},{11,10},{13,12},{... | collective-permute-start | bytes 786440 | tf_op jit(solution)/shard_map/ppermute | solution.py:346
  62.7 13.1 %all-to-all-start.3 = ((f32[32,1,256]{2,1,0:T(1,128)}), f32[32,1,256]{2,1,0:T(1,128)S(1)}, u32[]{:S(2)}, u32[]{:S(2)}) async-start(f32[32,1,256]{2,1,0:T(1,128)} %fold.3), calls=%async_computation.3 | async-start | bytes 65536 | tf_op jit(solution)/shard_map/all_to_all | solution.py:38

commit v7 on v6

--- a/solution.py
+++ b/solution.py
@@ -52,13 +52,16 @@
 
 def pack_kernel(key_ref, value_ref, place_ref, out_ref, row_ref, block_ref, in_sems, out_sems):
     rows = key_ref.shape[1]
-    fetches = [
-        pltpu.make_async_copy(place_ref, row_ref, in_sems.at[0]),
-        pltpu.make_async_copy(key_ref.at[0], block_ref.at[:, :KV_WIDTH], in_sems.at[1]),
-        pltpu.make_async_copy(
-            value_ref.at[0], block_ref.at[:, KV_WIDTH : 2 * KV_WIDTH], in_sems.at[2]
-        ),
-    ]
+    half = rows // 2
+    fetches = [pltpu.make_async_copy(place_ref, row_ref, in_sems.at[0])]
+    for top in (0, half):
+        for i, source in enumerate((key_ref, value_ref)):
+            target = block_ref.at[top : top + half, i * KV_WIDTH : (i + 1) * KV_WIDTH]
+            fetches.append(
+                pltpu.make_async_copy(
+                    source.at[0, top : top + half], target, in_sems.at[len(fetches)]
+                )
+            )
     for fetch in fetches:
         fetch.start()
     fetches[0].wait()
@@ -68,13 +71,15 @@
     lane = lax.broadcasted_iota(jnp.int32, (rows, 128), 1)
     coded = jnp.where(lane == 0, high, jnp.where(lane == 1, low, 0.0))
     block_ref[:, 2 * KV_WIDTH :] = coded.astype(jnp.bfloat16)
-    fetches[1].wait()
-    fetches[2].wait()
-    copies = [
-        pltpu.make_async_copy(block_ref, out_ref.at[part], out_sems.at[part]) for part in range(Y)
-    ]
-    for copy in copies:
-        copy.start()
+    copies = []
+    for step, top in enumerate((0, half)):
+        fetches[1 + 2 * step].wait()
+        fetches[2 + 2 * step].wait()
+        for part in range(Y):
+            source = block_ref.at[top : top + half]
+            target = out_ref.at[part, top : top + half]
+            copies.append(pltpu.make_async_copy(source, target, out_sems.at[step, part]))
+            copies[-1].start()
     for copy in copies:
         copy.wait()
 
@@ -161,8 +166,9 @@
     qp_ref,
     gate_ref,
     dq_ref,
-    *term_refs,
+    *refs,
 ):
+    *term_refs, bias_ref = refs
     rows = q_ref.shape[1]
     me = lax.axis_index("ctx")
     owners = [lax.rem(me + 2 * Y - back - Y_FIRST, Y) for back in range(Y)]
@@ -170,7 +176,11 @@
     def blocks(ref, columns):
         return jnp.concatenate([ref[owner, :, columns] for owner in owners], axis=0)
 
-    bias = mask_bias(key_places(blocks(kp_ref, slice(0, 128))), qp_ref[:, : 2 * rows])
+    @pl.when(pl.program_id(0) == 0)
+    def _():
+        bias_ref[...] = mask_bias(key_places(blocks(kp_ref, slice(0, 128))), qp_ref[:, : 2 * rows])
+
+    bias = bias_ref[...]
     gate = gate_ref[:, :1]
     for c in range(heads):
         queries = stack_heads(q_ref[0], c * GROUP, rows)
@@ -256,8 +266,8 @@
         scratch_shapes=[
             pltpu.VMEM((1, rows), jnp.int32),
             pltpu.VMEM((rows, 2 * KV_WIDTH + 128), jnp.bfloat16),
-            pltpu.SemaphoreType.DMA((3,)),
-            pltpu.SemaphoreType.DMA((Y,)),
+            pltpu.SemaphoreType.DMA((5,)),
+            pltpu.SemaphoreType.DMA((2, Y)),
         ],
         compiler_params=params(FULL_VMEM),
         name="pack",
@@ -320,6 +330,7 @@
             whole(rows, 128),
         ],
         out_specs=[wide_block] + [pl.BlockSpec((rows, 2 * span), lambda i: (0, i))] * Y,
+        scratch_shapes=[pltpu.VMEM((Y * rows, 2 * rows), jnp.float32)],
         compiler_params=params(BACKWARD_VMEM),
         cost_estimate=pl.CostEstimate(
             flops=10 * rows * width * Y * rows,

time: 76.9 us -> 77.1 us (level)
  no operation moved by 1% of the time
where the time goes in v7:
time: 77.1 us; the launch traced here: 76.6 us
  starting transfers between devices  46.5 us (60%)
  Pallas kernels  14.6 us (19%)
  waiting for transfers between devices  13.4 us (17%)
  between operations  1.41 us (2%)
    all_to_all x4, starting transfers between devices, exchange(): lax.all_to_all(parts, axis, 0, 0, axis_index_groups=[order], tiled=True)  42.6 us
    all_to_all x4, waiting for transfers between devices, exchange(): lax.all_to_all(parts, axis, 0, 0, axis_index_groups=[order], tiled=True)  10.1 us
    pallas_call x1, Pallas kernels, body(): pl.pallas_call(functools.partial(backward_kernel, heads), grid=(steps,),...  7.36 us
    ppermute x3, starting transfers between devices, body(): lax.ppermute(terms[back], 'ctx', [(i, i - back) for i in range(back, Y)])  3.86 us
    ppermute x3, waiting for transfers between devices, body(): lax.ppermute(terms[back], 'ctx', [(i, i - back) for i in range(back, Y)])  3.27 us
    pallas_call x1, Pallas kernels, body(): pl.pallas_call(pack_kernel, out_shape=jax.ShapeDtypeStruct((Y, rows, 2 *...  2.03 us
    pallas_call x1, Pallas kernels, body(): pl.pallas_call(forward_kernel, out_shape=jax.ShapeDtypeStruct((rows, 128)...  1.95 us
  transfers between devices with their start and end apart: 7, of which 3 were waited for; matrix products, arithmetic and copies ran while one was open for 0% of the time, Pallas kernels for 11%

profile of v7, /device:TPU:1, one launch (start us, length us, event | category | flops | bytes accessed | tf_op | source)
XLA Modules:
  0.0 76.6 jit_solution(17392491341002406350)
XLA Ops:
  0.6 2.0 %pack.1 = bf16[4,64,2176]{2,1,0:T(8,128)(2,1)} custom-call(bf16[1,64,1024]{2,1,0:T(8,128)(2,1)} %key_ref.1, bf16[1,64,1024]{2,1,0:T(8,128)(2,1)} %value_ref.1, s32[1,64]{1,0:T(1,128)} %place_ref.1), custom_call_target="tpu_custom_call" | custom-call | tf_op jit(solution)/shard_map/pack/pallas_call | solution.py:261
  2.7 0.0 copy-start.5
  2.7 0.0 copy-start.1
  2.7 0.0 copy-start.2
  2.7 5.2 %all-to-all-start = ((bf16[4,64,2176]{2,1,0:T(8,128)(2,1)}), bf16[4,64,2176]{2,1,0:T(8,128)(2,1)S(1)}, u32[]{:S(2)}, u32[]{:S(2)}) async-start(bf16[4,64,2176]{2,1,0:T(8,128)(2,1)} %pack.1), calls=%async_computation | async-start | bytes 2228224 | tf_op jit(solution)/shard_map/all_to_all | solution.py:38
  8.5 0.0 copy-done.5
  8.5 0.1 tile.13.qp_ref
  8.6 0.0 copy-start.4
  8.6 9.4 %all-to-all-done.pay_ref.k_ref.v_ref.kp_ref = bf16[4,64,2176]{2,1,0:T(8,128)(2,1)S(1)} async-done(((bf16[4,64,2176]{2,1,0:T(8,128)(2,1)}), bf16[4,64,2176]{2,1,0:T(8,128)(2,1)S(1)}, u32[]{:S(2)}, u32[]{:S(2)}) %all-to-all-start) | async-done | bytes 1114144 | tf_op jit(solution)/shard_map/all_to_all | solution.py:38
  18.0 0.0 copy-done.1
  18.0 0.0 copy-done.2
  18.0 0.0 copy-start
  18.0 0.0 copy-start.3
  18.1 2.0 %forward.1.along_ref = f32[64,128]{1,0:T(8,128)S(1)} custom-call(bf16[1,64,8192]{2,1,0:T(8,128)(2,1)S(1)} %copy-done.1, bf16[1,64,8192]{2,1,0:T(8,128)(2,1)S(1)} %copy-done.2, bf16[4,64,2176]{2,1,0:T(8,128)(2,1)S(1)} %all-to-all-done.pay_ref.k_ref.v_ref.kp_ref, s32[1,512]{1,0:T(1,128)S(1)} %tile.13.qp_ref), custom_call_target="tpu_custom_call" | custom-call | flops 536870912 | bytes 3145728 | tf_op jit(solution)/shard_map/forward/pallas_call | solution.py:289
  20.0 0.0 copy-done
  20.0 0.0 copy-done.4
  20.0 0.0 copy-done.3
  20.0 1.2 %router.1 = (f32[32,1,256]{2,1,0:T(1,128)}, f32[64,128]{1,0:T(8,128)S(1)}) custom-call(f32[64,128]{1,0:T(8,128)S(1)} %forward.1.along_ref, bf16[1,64,8192]{2,1,0:T(8,128)(2,1)S(1)} %copy-done.3, f32[1,8192]{1,0:T(1,128)S(1)} %bitcast.3, s32[1,1]{1,0:T(1,128)S(6)} %copy.13.count_ref), custom_call_target="tpu_custom_call" | custom-call | flops 2097152 | bytes 1048576 | tf_op jit(solution)/shard_map/router/pallas_call | solution.py:302
  21.2 12.8 %all-to-all-start.1 = ((f32[32,1,256]{2,1,0:T(1,128)}), f32[32,1,256]{2,1,0:T(1,128)S(1)}, u32[]{:S(2)}, u32[]{:S(2)}) async-start(f32[32,1,256]{2,1,0:T(1,128)} %get-tuple-element.22), calls=%async_computation.1 | async-start | bytes 65536 | tf_op jit(solution)/shard_map/all_to_all | solution.py:38
  34.1 7.4 %backward.1 = (bf16[1,64,8192]{2,1,0:T(8,128)(2,1)}, bf16[64,2048]{1,0:T(8,128)(2,1)S(1)}, bf16[64,2048]{1,0:T(8,128)(2,1)S(1)}, bf16[64,2048]{1,0:T(8,128)(2,1)S(1)}, bf16[64,2048]{1,0:T(8,128)(2,1)}) custom-call(bf16[1,64,8192]{2,1,0:T(8,128)(2,1)} %q_ref.3, bf16[1,64,8192]{2,1,0:T(8,128)(2,1)} %grad_ref.3, bf16[4,64,2176]{2,1,0:T(8,128)(2,1)} %copy-done, ...), custom_call_target="tpu_custom_call" | custom-call | flops 1342177280 | bytes 3145728 | tf_op jit(solution)/shard_map/backward/pallas_call | solution.py:316
  41.4 0.0 all-to-all-done.1.share_ref
  41.4 0.6 fold.2
  42.1 15.6 %all-to-all-start.2 = ((f32[16,1,256]{2,1,0:T(1,128)}), f32[16,1,256]{2,1,0:T(1,128)S(1)}, u32[]{:S(2)}, u32[]{:S(2)}) async-start(f32[16,1,256]{2,1,0:T(1,128)} %fold.2), calls=%async_computation.2 | async-start | bytes 32768 | tf_op jit(solution)/shard_map/all_to_all | solution.py:38
  57.7 1.3 %collective-permute-start = (bf16[64,2048]{1,0:T(8,128)(2,1)S(1)}, bf16[64,2048]{1,0:T(8,128)(2,1)S(1)}, u32[]{:S(2)}, u32[]{:S(2)}) collective-permute-start(bf16[64,2048]{1,0:T(8,128)(2,1)S(1)} %get-tuple-element.29), channel_id=1, source_target_pairs={{2,0},{3,1},{6,4},{7,5},{10,8},{11,9},{14,12},{15,13},{18,16},{19,... | collective-permute-start | bytes 786440 | tf_op jit(solution)/shard_map/ppermute | solution.py:357
  58.9 1.3 %collective-permute-start.1 = (bf16[64,2048]{1,0:T(8,128)(2,1)}, bf16[64,2048]{1,0:T(8,128)(2,1)S(1)}, u32[]{:S(2)}, u32[]{:S(2)}) collective-permute-start(bf16[64,2048]{1,0:T(8,128)(2,1)} %get-tuple-element.30), channel_id=1, source_target_pairs={{3,0},{7,4},{11,8},{15,12},{19,16},{23,20},{27,24},{31,28},{35,32}... | collective-permute-start | bytes 786440 | tf_op jit(solution)/shard_map/ppermute | solution.py:357
  60.2 1.3 %collective-permute-start.2 = (bf16[64,2048]{1,0:T(8,128)(2,1)S(1)}, bf16[64,2048]{1,0:T(8,128)(2,1)S(1)}, u32[]{:S(2)}, u32[]{:S(2)}) collective-permute-start(bf16[64,2048]{1,0:T(8,128)(2,1)S(1)} %get-tuple-element.31), channel_id=1, source_target_pairs={{1,0},{2,1},{3,2},{5,4},{6,5},{7,6},{9,8},{10,9},{11,10},{13,12},{... | collective-permute-start | bytes 786440 | tf_op jit(solution)/shard_map/ppermute | solution.py:357
  61.5 0.7 all-to-all-done.2.share_ref
  62.2 0.6 fold.3
  62.9 9.0 %all-to-all-start.3 = ((f32[32,1,256]{2,1,0:T(1,128)}), f32[32,1,256]{2,1,0:T(1,128)S(1)}, u32[]{:S(2)}, u32[]{:S(2)}) async-start(f32[32,1,256]{2,1,0:T(1,128)} %fold.3), calls=%async_computation.3 | async-start | bytes 65536 | tf_op jit(solution)/shard_map/all_to_all | solution.py:38
  71.9 0.0 collective-permute-done.refs_1_
  71.9 3.3 %collective-permute-done.1.refs_2_ = bf16[64,2048]{1,0:T(8,128)(2,1)S(1)} collective-permute-done((bf16[64,2048]{1,0:T(8,128)(2,1)}, bf16[64,2048]{1,0:T(8,128)(2,1)S(1)}, u32[]{:S(2)}, u32[]{:S(2)}) %collective-permute-start.1) | collective-permute-done | bytes 262176 | tf_op jit(solution)/shard_map/ppermute | solution.py:357
  75.2 0.0 collective-permute-done.2.refs_3_
  75.2 0.8 %combine.1 = (bf16[1,64,1024]{2,1,0:T(8,128)(2,1)}, bf16[1,64,1024]{2,1,0:T(8,128)(2,1)}) custom-call(bf16[64,2048]{1,0:T(8,128)(2,1)S(1)} %get-tuple-element.28.refs_0_, bf16[64,2048]{1,0:T(8,128)(2,1)S(1)} %collective-permute-done.refs_1_, bf16[64,2048]{1,0:T(8,128)(2,1)S(1)} %collective-permute-done.1.refs_2_, ...), custom_call_target="tpu_custom_call" | custom-call | flops 262144 | bytes 1310720 | tf_op jit(solution)/shard_map/combine/pallas_call | solution.py:362
  76.0 0.0 all-to-all-done.3
  76.0 0.6 copy.14
  (1 shorter events, 0.0 us)
Async XLA Ops:
  2.7 5.8 %copy-start.5 = (s32[1,64]{1,0:T(1,128)S(1)}, s32[1,64]{1,0:T(1,128)}, u32[]{:S(2)}) copy-start(s32[1,64]{1,0:T(1,128)} %place_ref.1) | copy-start | bytes 772
  2.7 15.4 %copy-start.1 = (bf16[1,64,8192]{2,1,0:T(8,128)(2,1)S(1)}, bf16[1,64,8192]{2,1,0:T(8,128)(2,1)}, u32[]{:S(2)}) copy-start(bf16[1,64,8192]{2,1,0:T(8,128)(2,1)} %q_ref.3) | copy-start | bytes 3145732
  2.7 15.4 %copy-start.2 = (bf16[1,64,8192]{2,1,0:T(8,128)(2,1)S(1)}, bf16[1,64,8192]{2,1,0:T(8,128)(2,1)}, u32[]{:S(2)}) copy-start(bf16[1,64,8192]{2,1,0:T(8,128)(2,1)} %grad_ref.3) | copy-start | bytes 3145732
  2.7 15.3 %all-to-all-start = ((bf16[4,64,2176]{2,1,0:T(8,128)(2,1)}), bf16[4,64,2176]{2,1,0:T(8,128)(2,1)S(1)}, u32[]{:S(2)}, u32[]{:S(2)}) async-start(bf16[4,64,2176]{2,1,0:T(8,128)(2,1)} %pack.1), calls=%async_computation | async-start | bytes 2228224 | tf_op jit(solution)/shard_map/all_to_all | solution.py:38
  8.6 11.4 %copy-start.4 = (f32[8192]{0:T(1024)S(1)}, f32[8192]{0:T(1024)}, u32[]{:S(2)}) copy-start(f32[8192]{0:T(1024)} %param.15) | copy-start | bytes 98308
  18.0 2.0 %copy-start = (bf16[4,64,2176]{2,1,0:T(8,128)(2,1)}, bf16[4,64,2176]{2,1,0:T(8,128)(2,1)S(1)}, u32[]{:S(2)}) copy-start(bf16[4,64,2176]{2,1,0:T(8,128)(2,1)S(1)} %all-to-all-done.pay_ref.k_ref.v_ref.kp_ref) | copy-start | bytes 3342340
  18.0 2.0 %copy-start.3 = (bf16[1,64,8192]{2,1,0:T(8,128)(2,1)S(1)}, bf16[1,64,8192]{2,1,0:T(8,128)(2,1)}, u32[]{:S(2)}) copy-start(bf16[1,64,8192]{2,1,0:T(8,128)(2,1)} %hidden_ref.1) | copy-start | bytes 3145732
  21.2 20.2 %all-to-all-start.1 = ((f32[32,1,256]{2,1,0:T(1,128)}), f32[32,1,256]{2,1,0:T(1,128)S(1)}, u32[]{:S(2)}, u32[]{:S(2)}) async-start(f32[32,1,256]{2,1,0:T(1,128)} %get-tuple-element.22), calls=%async_computation.1 | async-start | bytes 65536 | tf_op jit(solution)/shard_map/all_to_all | solution.py:38
  42.1 20.1 %all-to-all-start.2 = ((f32[16,1,256]{2,1,0:T(1,128)}), f32[16,1,256]{2,1,0:T(1,128)S(1)}, u32[]{:S(2)}, u32[]{:S(2)}) async-start(f32[16,1,256]{2,1,0:T(1,128)} %fold.2), calls=%async_computation.2 | async-start | bytes 32768 | tf_op jit(solution)/shard_map/all_to_all | solution.py:38
  57.7 14.3 %collective-permute-start = (bf16[64,2048]{1,0:T(8,128)(2,1)S(1)}, bf16[64,2048]{1,0:T(8,128)(2,1)S(1)}, u32[]{:S(2)}, u32[]{:S(2)}) collective-permute-start(bf16[64,2048]{1,0:T(8,128)(2,1)S(1)} %get-tuple-element.29), channel_id=1, source_target_pairs={{2,0},{3,1},{6,4},{7,5},{10,8},{11,9},{14,12},{15,13},{18,16},{19,... | collective-permute-start | bytes 786440 | tf_op jit(solution)/shard_map/ppermute | solution.py:357
  58.9 16.2 %collective-permute-start.1 = (bf16[64,2048]{1,0:T(8,128)(2,1)}, bf16[64,2048]{1,0:T(8,128)(2,1)S(1)}, u32[]{:S(2)}, u32[]{:S(2)}) collective-permute-start(bf16[64,2048]{1,0:T(8,128)(2,1)} %get-tuple-element.30), channel_id=1, source_target_pairs={{3,0},{7,4},{11,8},{15,12},{19,16},{23,20},{27,24},{31,28},{35,32}... | collective-permute-start | bytes 786440 | tf_op jit(solution)/shard_map/ppermute | solution.py:357
  60.2 14.9 %collective-permute-start.2 = (bf16[64,2048]{1,0:T(8,128)(2,1)S(1)}, bf16[64,2048]{1,0:T(8,128)(2,1)S(1)}, u32[]{:S(2)}, u32[]{:S(2)}) collective-permute-start(bf16[64,2048]{1,0:T(8,128)(2,1)S(1)} %get-tuple-element.31), channel_id=1, source_target_pairs={{1,0},{2,1},{3,2},{5,4},{6,5},{7,6},{9,8},{10,9},{11,10},{13,12},{... | collective-permute-start | bytes 786440 | tf_op jit(solution)/shard_map/ppermute | solution.py:357
  62.9 13.1 %all-to-all-start.3 = ((f32[32,1,256]{2,1,0:T(1,128)}), f32[32,1,256]{2,1,0:T(1,128)S(1)}, u32[]{:S(2)}, u32[]{:S(2)}) async-start(f32[32,1,256]{2,1,0:T(1,128)} %fold.3), calls=%async_computation.3 | async-start | bytes 65536 | tf_op jit(solution)/shard_map/all_to_all | solution.py:38
